TPU v7x, 32 devices: a whole 2x2x4 slice. The times are simulated.
32 devices in a mesh: seq: 4 (over y, x), tensor: 8 (over z, core).
Axes of the slice: x: 2, y: 2, z: 4, core: 2. Of those that a mesh axis runs over, the one named last changes fastest.
Arguments:
- hidden_in: bfloat16 [4096, 2304], P(('seq', 'tensor')), may hold values from -6 to 6
- norm_attn: float32 [2304], replicated, may hold values from 0.1 to 1.9
- norm_ffn: float32 [2304], replicated, may hold values from 0.1 to 1.9
- w_qkv: bfloat16 [3, 2304, 512], P(None, None, 'tensor'), may hold values from -1 to 1
- w_out: bfloat16 [512, 2304], P('tensor'), may hold values from -0.25 to 0.25
- w_router: float32 [2304, 8], replicated, may hold values from -4 to 4
- w_gate_up: bfloat16 [2, 23040, 2304], P(None, 'tensor'), may hold values from -0.125 to 0.125
- w_down: bfloat16 [23040, 2304], P('tensor'), may hold values from -0.109375 to 0.109375
- segment_ids: int32 [4096], P('seq'), may hold values from 0 to 7, never falling along the last dimension, each value on 1 to 3072 neighbouring positions
- expert_ids: int32 [4096, 2], P(('seq', 'tensor')), may hold values from 0 to 7, all different within a row; in each aligned block of 128 rows (0 to 127, 128 to 255, ...) at most 64 rows name the same one
Outputs:
- hidden_out: bfloat16 [4096, 2304], P(('seq', 'tensor'))
- kv_cache: bfloat16 [8, 4096, 128], P('tensor', 'seq')
Inputs may be any that keep to these rules, and one draw needn't show every extreme that they name: `segment_ids`: nondecreasing along the stream; each prompt has 1 to 3072 tokens and one has exactly 3072. `expert_ids`: the two experts of a token differ. Within each aligned block of 128 tokens (the tokens of one device), no expert is named by more than 64 tokens, a bound that some block reaches.
All inputs are finite; a program needn't handle non-finite values.
Results may differ from a plain program's by a relative error of at most 0.019.
Values may be sent and summed in bfloat16 or wider, within the bound.
A program may use at most 128 MiB of HBM per device.

v0:
```python
import math

import jax
import jax.numpy as jnp
from jax import lax
from jax.sharding import PartitionSpec as P

HD = 64


epsilon = 1e-06
low_score = -1e30


def rms_norm(hidden_rows, gain):
    as_float = hidden_rows.astype(jnp.float32)
    scale = lax.rsqrt(jnp.mean(as_float * as_float, axis=-1, keepdims=True) + epsilon)
    return (as_float * scale * gain).astype(jnp.bfloat16)


def rotate(head_rows, positions):
    half_size = head_rows.shape[-1] // 2
    frequency = jnp.exp(jnp.arange(half_size, dtype=jnp.float32) * (-math.log(10000.0) / half_size))
    angles = positions.astype(jnp.float32)[:, None] * frequency[None, :]
    cosine = jnp.cos(angles)[:, None, :]
    sine_part = jnp.sin(angles)[:, None, :]
    front_half = head_rows[..., :half_size]
    back_half = head_rows[..., half_size:]
    return jnp.concatenate(
        [front_half * cosine - back_half * sine_part, back_half * cosine + front_half * sine_part],
        axis=-1,
    )


def fold_keys(
    softmax_state, query_rows, query_segments, query_positions, kv_rows, key_segments, key_start
):
    running_max, denominator, weighted_sum = softmax_state
    row_count = kv_rows.shape[0]
    block_size = math.gcd(row_count, 2048)
    head_size = query_rows.shape[-1]
    for block_start in range(0, row_count, block_size):
        kv_block = kv_rows[block_start : block_start + block_size]
        key_block = kv_block[..., :head_size]
        value_block = kv_block[..., head_size:]
        segment_block = key_segments[block_start : block_start + block_size]
        position_block = key_start + block_start + jnp.arange(block_size, dtype=jnp.int32)
        scores = (
            jnp.einsum("qhd,khd->hqk", query_rows, key_block, preferred_element_type=jnp.float32)
            * 0.125
        )
        allowed = (query_segments[:, None] == segment_block[None, :]) & (
            position_block[None, :] <= query_positions[:, None]
        )
        masked = jnp.where(allowed[None], scores, low_score)
        new_max = jnp.maximum(running_max, jnp.max(masked, axis=-1))
        weights = jnp.where(allowed[None], jnp.exp(masked - new_max[..., None]), 0.0)
        factor = jnp.exp(running_max - new_max)
        denominator = denominator * factor + jnp.sum(weights, axis=-1)
        weighted_sum = weighted_sum * factor[..., None] + jnp.einsum(
            "hqk,khd->hqd",
            weights.astype(jnp.bfloat16),
            value_block,
            preferred_element_type=jnp.float32,
        )
        running_max = new_max
    return (running_max, denominator, weighted_sum)


def slot_table(token_ids, target, slot_count):
    is_routed = jnp.any(token_ids == target, axis=1).astype(jnp.int32)
    slot_rank = jnp.cumsum(is_routed) - 1
    chosen_slot = (is_routed[None, :] == 1) & (
        slot_rank[None, :] == jnp.arange(slot_count, dtype=jnp.int32)[:, None]
    )
    return chosen_slot.astype(jnp.bfloat16)


def expert_apply(slot_rows, slot_ids, own_expert, w_router, w_gate_up, w_down):
    logits = jnp.dot(slot_rows.astype(jnp.float32), w_router, precision=lax.Precision.HIGHEST)
    expert_count = w_router.shape[1]
    one_hot = (
        slot_ids[:, :, None] == jnp.arange(expert_count, dtype=jnp.int32)[None, None, :]
    ).astype(jnp.float32)
    chosen = jnp.sum(one_hot * logits[:, None, :], axis=-1)
    gate_probs = jax.nn.softmax(chosen, axis=-1)
    weight = jnp.sum(jnp.where(slot_ids == own_expert, gate_probs, 0.0), axis=-1)
    contract = (((1,), (1,)), ((), ()))
    gate_act = lax.dot_general(
        slot_rows, w_gate_up[0], contract, preferred_element_type=jnp.float32
    )
    up_act = lax.dot_general(slot_rows, w_gate_up[1], contract, preferred_element_type=jnp.float32)
    hidden_act = (jax.nn.silu(gate_act) * up_act).astype(jnp.bfloat16)
    output = jnp.dot(hidden_act, w_down, preferred_element_type=jnp.float32)
    return (output * weight[:, None]).astype(jnp.bfloat16)


def shards(
    hidden_in,
    norm_attn,
    norm_ffn,
    w_qkv,
    w_out,
    w_router,
    w_gate_up,
    w_down,
    segment_ids,
    expert_ids,
):
    local_rows = hidden_in.shape[0]
    model_width = hidden_in.shape[1]
    tensor_count = lax.axis_size("tensor")
    tensor_place = lax.axis_index("tensor")
    seq_place = lax.axis_index("seq")
    group_rows = local_rows * tensor_count
    head_count = w_qkv.shape[2] // HD
    normed = rms_norm(hidden_in, norm_attn)
    projected = jnp.einsum(
        "td,cdh->tch",
        lax.all_gather(normed, "tensor", axis=0, tiled=True),
        w_qkv,
        preferred_element_type=jnp.float32,
    )
    positions = seq_place * group_rows + jnp.arange(group_rows, dtype=jnp.int32)
    query_rows = rotate(projected[:, 0].reshape(group_rows, head_count, HD), positions).astype(
        jnp.bfloat16
    )
    key_rows = rotate(projected[:, 1].reshape(group_rows, head_count, HD), positions).astype(
        jnp.bfloat16
    )
    value_rows = projected[:, 2].reshape(group_rows, head_count, HD).astype(jnp.bfloat16)
    kv_rows = jnp.concatenate([key_rows, value_rows], axis=-1)
    kv_cache = kv_rows.transpose(1, 0, 2)
    start_state = (
        jnp.full((head_count, group_rows), low_score, jnp.float32),
        jnp.zeros((head_count, group_rows), jnp.float32),
        jnp.zeros((head_count, group_rows, HD), jnp.float32),
    )
    softmax_state = fold_keys(
        start_state,
        query_rows,
        segment_ids,
        positions,
        lax.all_gather(kv_rows, "seq", axis=0, tiled=True),
        lax.all_gather(segment_ids, "seq", axis=0, tiled=True),
        jnp.int32(0),
    )
    running_max, denominator, weighted_sum = softmax_state
    attended = (
        (weighted_sum / denominator[..., None])
        .transpose(1, 0, 2)
        .reshape(group_rows, head_count * HD)
        .astype(jnp.bfloat16)
    )
    attention_sum = lax.psum_scatter(
        jnp.dot(attended, w_out, preferred_element_type=jnp.float32).astype(jnp.bfloat16),
        "tensor",
        scatter_dimension=0,
        tiled=True,
    ).astype(jnp.float32)
    residual = hidden_in.astype(jnp.float32) + attention_sum
    normed_ffn = rms_norm(residual, norm_ffn)
    expert_count = w_router.shape[1]
    slice_count = tensor_count // expert_count
    own_expert = tensor_place // slice_count
    slot_count = local_rows // 2
    full_rows, full_ids = (
        lax.all_gather(normed_ffn, "tensor", axis=0, tiled=True),
        lax.all_gather(expert_ids, "tensor", axis=0, tiled=True),
    )
    block_ids = full_ids.reshape(tensor_count, local_rows, 2)
    slot_tables = jax.vmap(lambda source_ids: slot_table(source_ids, own_expert, slot_count))(
        block_ids
    )
    slot_rows = jnp.einsum(
        "sjr,srd->sjd",
        slot_tables,
        full_rows.reshape(tensor_count, local_rows, model_width),
        preferred_element_type=jnp.float32,
    ).astype(jnp.bfloat16)
    slot_ids = jnp.einsum(
        "sjr,srk->sjk", slot_tables.astype(jnp.float32), block_ids.astype(jnp.float32)
    ).astype(jnp.int32)
    term_rows = expert_apply(
        slot_rows.reshape(-1, model_width),
        slot_ids.reshape(-1, 2),
        own_expert,
        w_router,
        w_gate_up,
        w_down,
    )
    placed = jnp.einsum(
        "sjr,sjd->srd",
        slot_tables,
        term_rows.reshape(tensor_count, slot_count, model_width),
        preferred_element_type=jnp.float32,
    ).reshape(group_rows, model_width)
    expert_sum = lax.psum_scatter(
        placed.astype(jnp.bfloat16), "tensor", scatter_dimension=0, tiled=True
    ).astype(jnp.float32)
    hidden_out = (residual + expert_sum).astype(jnp.bfloat16)
    return (hidden_out, kv_cache)


def solution(mesh):
    placed = (
        P(("seq", "tensor"), None),
        P(),
        P(),
        P(None, None, "tensor"),
        P("tensor", None),
        P(),
        P(None, "tensor", None),
        P("tensor", None),
        P("seq"),
        P(("seq", "tensor"), None),
    )
    return jax.shard_map(
        shards,
        mesh=mesh,
        in_specs=placed,
        out_specs=(P(("seq", "tensor"), None), P("tensor", "seq", None)),
        check_vma=False,
    )
```

profile of v0, /device:TPU:0, one launch (start us, length us, event | category | flops | bytes accessed | tf_op | source)
XLA Modules:
  0.0 339.1 jit_solution(3009074950179447410)
XLA Ops:
  7.2 1.3 fusion.20
  8.6 2.1 fusion.22
  10.8 54.5 %all-gather.4.cloned.1.call-done = bf16[1024,2304]{1,0:T(8,128)(2,1)} async-done(((bf16[128,2304]{1,0:T(8,128)(2,1)}), bf16[1024,2304]{1,0:T(8,128)(2,1)}) %all-gather.4.cloned.1.call-update) | async-done | bytes 4718608 | tf_op jit(solution)/shard_map/all_gather | solution.py:120
  65.3 4.0 %fusion.95 = f32[1024,192]{0,1:S(1)} fusion(bf16[1024,2304]{1,0:T(8,128)(2,1)} %all-gather.4.cloned.1.call-done, bf16[2304,192]{0,1:T(8,128)(2,1)S(1)} %bitcast.62), kind=kOutput, calls=%fused_computation.118 | convolution fusion | flops 905969664 | bytes 6389760
  70.7 8.1 %all_gather.15 = s32[4096]{0:T(1024)S(1)} all-gather(s32[1024]{0:T(1024)S(1)} %copy-done.8), channel_id=1, replica_groups=mesh['seq'=4,'tensor'=8] {'seq'}, dimensions={0}, use_global_device_ids=true | all-gather | bytes 20480 | tf_op jit(solution)/shard_map/all_gather | solution.py:145
  78.9 17.4 %all-gather.6.cloned.1.call-done = bf16[4096,1,128]{0,2,1:T(8,128)(2,1)} async-done(((bf16[1024,1,128]{0,2,1:T(8,128)(2,1)}), bf16[4096,1,128]{0,2,1:T(8,128)(2,1)}) %all-gather.6.cloned.1.call-update) | async-done | bytes 1048592 | tf_op jit(solution)/shard_map/all_gather | solution.py:144
  96.3 2.3 fusion.41
  98.6 4.1 %fusion.8 = (f32[1024]{0:T(1024)S(1)}, f32[1024]{0:T(1024)S(1)}, f32[1024,2048]{1,0:T(8,128)S(1)}) fusion(s32[2048]{0:T(1024)S(1)} %iota_add_fusion, s32[2048]{0:T(1024)S(1)} %get-tuple-element.23, s32[1024]{0:T(1024)S(1)} %iota_add_fusion.1, s32[1024]{0:T(1024)S(1)} %copy-done.8, f32[1024,2048]{1,0:T(8,128)S(1)} %fusion.41, ...), kind=kOutput, calls=%fused_computation.14 | convolution fusion | flops 293861376 | bytes 17211392 | tf_op jit(solution)/shard_map/qhd,khd->hqk/dot_general | solution.py:49
  102.7 6.2 %fusion.12 = (f32[1024]{0:T(1024)S(1)}, f32[1024]{0:T(1024)S(1)}) fusion(f32[1024,2048]{1,0:T(8,128)S(1)} %fusion.41, f32[1024]{0:T(1024)S(1)} %get-tuple-element.26, s32[2048]{0:T(1024)S(1)} %get-tuple-element.22, s32[1024]{0:T(1024)S(1)} %iota_add_fusion.1, s32[1024]{0:T(1024)S(1)} %copy-done.8, f32[1024]{0:T(1024)S(1)} %get-tuple-element.25, ...), kind=kLoop, calls=%fused_computation.21 | loop fusion | flops 33552384 | bytes 16826368 | tf_op jit(solution)/shard_map/reduce_sum | solution.py:59
  108.9 2.7 fusion.29
  111.7 8.0 %convolution_convert_fusion.1 = bf16[1024,2304]{1,0:T(8,128)(2,1)} fusion(bf16[64,2304]{1,0:T(8,128)(2,1)S(1)} %copy-done.11, f32[1024,64]{0,1:T(8,128)S(1)} %fusion.29, f32[1024,2048]{1,0:T(8,128)} %copy-done.4, f32[1024]{0:T(1024)S(1)} %get-tuple-element.25, s32[2048]{0:T(1024)S(1)} %iota_add_fusion, s32[2048]{0:T(1024)S(1)} %get-tuple-element.23, ...), kind=kOutput, calls=%fused_computation.17 | convolution fusion | flops 589758464 | bytes 13959168 | tf_op jit(solution)/shard_map/dot_general | solution.py:156
  120.0 54.9 %reduce-scatter.3.cloned.1.call-done = bf16[128,2304]{1,0:T(8,128)(2,1)} async-done(((bf16[1024,2304]{1,0:T(8,128)(2,1)}), bf16[128,2304]{1,0:T(8,128)(2,1)}) %reduce-scatter.3.cloned.1.call-update) | async-done | bytes 589840 | tf_op jit(solution)/shard_map/reduce_scatter | solution.py:155
  174.9 1.3 multiply_reduce_fusion
  176.2 2.1 multiply_convert_fusion.1
  178.4 9.2 %all_gather.18 = s32[1024,2]{0,1:T(2,128)S(1)} all-gather(s32[128,2]{0,1:T(2,128)S(1)} %copy-done.10), channel_id=1, replica_groups=mesh['seq'=4,'tensor'=8] {'tensor'}, dimensions={0}, use_global_device_ids=true | all-gather | bytes 9216 | tf_op jit(solution)/shard_map/all_gather | solution.py:169
  188.2 40.4 %all-gather.8.cloned.1.call-done = bf16[1024,2304]{1,0:T(8,128)(2,1)} async-done(((bf16[128,2304]{1,0:T(8,128)(2,1)}), bf16[1024,2304]{1,0:T(8,128)(2,1)}) %all-gather.8.cloned.1.call-update) | async-done | bytes 4718608 | tf_op jit(solution)/shard_map/all_gather | solution.py:168
  228.6 3.1 convolution_convert_fusion.2
  231.7 1.5 copy-done.3
  233.2 1.9 fusion.96
  235.3 12.5 %fusion.2 = f32[512,2880]{0,1:T(8,128)} fusion(bf16[512,2304]{1,0:T(8,128)(2,1)} %bitcast.65, bf16[2,2880,2304]{2,1,0:T(8,128)(2,1)} %param.16), kind=kOutput, calls=%fused_computation.2 | convolution fusion | flops 6794772480 | bytes 21528576 | tf_op jit(solution)/shard_map/dot_general | solution.py:89
  248.0 23.2 %fusion.11 = bf16[512,2304]{1,0:T(8,128)(2,1)} fusion(bf16[2880,2304]{1,0:T(8,128)(2,1)} %param.17, f32[512]{0:T(512)S(1)} %mul.193, f32[512,2880]{0,1:T(8,128)} %fusion.2, bf16[512,2304]{1,0:T(8,128)(2,1)} %bitcast.66, bf16[2,2880,2304]{2,1,0:T(8,128)(2,1)} %param.16), kind=kOutput, calls=%fused_computation.20 | convolution fusion | flops 13600751616 | bytes 37160960 | tf_op jit(solution)/shard_map/dot_general | solution.py:94
  271.2 5.3 %convolution_convert_fusion = bf16[8,128,2304]{2,1,0:T(8,128)(2,1)} fusion(bf16[8,64,2304]{2,1,0:T(8,128)(2,1)} %bitcast.68, s32[8,128]{1,0:T(8,128)S(1)} %broadcast_add_fusion, pred[8,128]{1,0:T(8,128)(4,1)S(1)} %broadcast_compare_fusion), kind=kOutput, calls=%fused_computation.16 | convolution fusion | flops 304480256 | bytes 7083008 | tf_op jit(solution)/shard_map/sjr,sjd->srd/dot_general | solution.py:192
  277.4 53.1 %reduce-scatter.5.cloned.1.call-done = bf16[128,2304]{1,0:T(8,128)(2,1)} async-done(((bf16[1024,2304]{1,0:T(8,128)(2,1)}), bf16[128,2304]{1,0:T(8,128)(2,1)}) %reduce-scatter.5.cloned.1.call-update) | async-done | bytes 589840 | tf_op jit(solution)/shard_map/reduce_scatter | solution.py:198
  330.5 2.1 add_convert_fusion
  (62 shorter events, 3.8 us)
Async XLA Ops:
  7.2 58.1 %copy-start = (bf16[3,2304,64]{1,2,0:T(8,128)(2,1)S(1)}, bf16[3,2304,64]{1,2,0:T(8,128)(2,1)}, u32[]{:S(2)}) copy-start(bf16[3,2304,64]{1,2,0:T(8,128)(2,1)} %param.13) | copy-start | bytes 2654212
  7.2 63.5 %copy-start.8 = (s32[1024]{0:T(1024)S(1)}, s32[1024]{0:T(1024)}, u32[]{:S(2)}) copy-start(s32[1024]{0:T(1024)} %param.18) | copy-start | bytes 12292
  7.2 58.1 %all-gather.4.cloned.1.call-start = ((), (), s32[]{:S(2)}) async-start(), calls=%async_computation.2 | async-start | bytes 5308416 | tf_op jit(solution)/shard_map/all_gather | solution.py:120
  10.7 85.6 %all-gather.6.cloned.1.call-start = ((), (), s32[]{:S(2)}) async-start(), calls=%async_computation.3 | async-start | bytes 1310720 | tf_op jit(solution)/shard_map/all_gather | solution.py:144
  70.7 104.2 %reduce-scatter.3.cloned.1.call-start = ((), (), s32[]{:S(2)}) async-start(), calls=%async_computation.4 | async-start | bytes 5308416 | tf_op jit(solution)/shard_map/reduce_scatter | solution.py:155
  96.3 2.3 copy-start.7
  102.7 6.2 %copy-start.4 = (f32[1024,2048]{1,0:T(8,128)}, f32[1024,2048]{1,0:T(8,128)S(1)}, u32[]{:S(2)}) copy-start(f32[1024,2048]{1,0:T(8,128)S(1)} %get-tuple-element.27) | copy-start | bytes 25165828
  108.9 2.8 copy-start.11
  111.7 63.2 %copy-start.2 = (bf16[128,2304]{1,0:T(8,128)(2,1)S(1)}, bf16[128,2304]{1,0:T(8,128)(2,1)}, u32[]{:S(2)}) copy-start(bf16[128,2304]{1,0:T(8,128)(2,1)} %param.10) | copy-start | bytes 1769476
  119.7 56.5 %copy-start.9 = (f32[2304]{0:T(1024)S(1)}, f32[2304]{0:T(1024)}, u32[]{:S(2)}) copy-start(f32[2304]{0:T(1024)} %param.12) | copy-start | bytes 27652
  119.7 58.7 %copy-start.10 = (s32[128,2]{0,1:T(2,128)S(1)}, s32[128,2]{0,1:T(2,128)}, u32[]{:S(2)}) copy-start(s32[128,2]{0,1:T(2,128)} %param.19) | copy-start | bytes 3076
  119.8 113.4 %copy-start.6 = (f32[2304,8]{0,1:T(8,128)S(1)}, f32[2304,8]{0,1:T(8,128)}, u32[]{:S(2)}) copy-start(f32[2304,8]{0,1:T(8,128)} %param.15) | copy-start | bytes 221188
  119.8 108.8 %all-gather.8.cloned.1.call-start = ((), (), s32[]{:S(2)}) async-start(), calls=%async_computation.5 | async-start | bytes 5308416 | tf_op jit(solution)/shard_map/all_gather | solution.py:168
  178.4 152.1 %reduce-scatter.5.cloned.1.call-start = ((), (), s32[]{:S(2)}) async-start(), calls=%async_computation.6 | async-start | bytes 5308416 | tf_op jit(solution)/shard_map/reduce_scatter | solution.py:198
  231.7 1.5 copy-start.3
  271.2 61.4 %copy-start.1 = (bf16[3,2304,64]{1,2,0:T(8,128)(2,1)S(1)}, bf16[3,2304,64]{1,2,0:T(8,128)(2,1)}, u32[]{:S(2)}) copy-start(bf16[3,2304,64]{1,2,0:T(8,128)(2,1)} %param.13) | copy-start | bytes 2654212
  271.2 59.3 %copy-start.5 = (bf16[128,2304]{1,0:T(8,128)(2,1)S(1)}, bf16[128,2304]{1,0:T(8,128)(2,1)}, u32[]{:S(2)}) copy-start(bf16[128,2304]{1,0:T(8,128)(2,1)} %reduce-scatter.3.cloned.1.call-done) | copy-start | bytes 1769476
Sparse Core Ops, SparseCore 0:
  10.8 54.3 all-gather.3
  70.8 25.4 all-gather.5
  119.9 54.9 reduce-scatter.2
  178.5 50.0 all-gather.7
  276.7 53.7 reduce-scatter.4
where the time goes:
time: 340 us; the launch traced here: 339 us
  waiting for transfers between devices  220 us (65%)
  matrix products  67.4 us (20%)
  blocking collectives  17.3 us (5%)
  other arithmetic  17 us (5%)
  between operations  14 us (4%)
    reduce_scatter x1, waiting for transfers between devices, shards(): lax.psum_scatter(jnp.dot(attended, w_out, preferred_element_type=jnp.floa...  54.9 us
    all_gather x1, waiting for transfers between devices, shards(): lax.all_gather(normed, 'tensor', axis=0, tiled=True)  54.5 us
    reduce_scatter x1, waiting for transfers between devices, shards(): lax.psum_scatter(placed.astype(jnp.bfloat16), 'tensor', scatter_dimension...  53.1 us
    all_gather x1, waiting for transfers between devices, shards(): lax.all_gather(normed_ffn, 'tensor', axis=0, tiled=True)  40.4 us
    dot_general x1, matrix products, expert_apply(): output = jnp.dot(hidden_act, w_down, preferred_element_type=jnp.float32)  23.2 us
    all_gather x1, waiting for transfers between devices, shards(): lax.all_gather(kv_rows, 'seq', axis=0, tiled=True)  17.4 us
    dot_general x1, matrix products, expert_apply(): lax.dot_general(slot_rows, w_gate_up[0], contract, preferred_element_type...  12.5 us
    all_gather x1, blocking collectives, shards(): lax.all_gather(expert_ids, 'tensor', axis=0, tiled=True)  9.15 us
  transfers between devices with their start and end apart: 5, of which 5 were waited for; matrix products, arithmetic and copies ran while one was open for 0% of the time, Pallas kernels for 0%

commit v1 on v0

--- a/solution.py
+++ b/solution.py
@@ -69,7 +69,8 @@
 
 def slot_table(token_ids, target, slot_count):
     is_routed = jnp.any(token_ids == target, axis=1).astype(jnp.int32)
-    slot_rank = jnp.cumsum(is_routed) - 1
+    places = jnp.arange(is_routed.shape[0], dtype=jnp.int32)
+    slot_rank = jnp.sum(jnp.where(places[None, :] <= places[:, None], is_routed[None, :], 0), axis=1) - 1
     chosen_slot = (is_routed[None, :] == 1) & (
         slot_rank[None, :] == jnp.arange(slot_count, dtype=jnp.int32)[:, None]
     )

time: 340 us -> 340 us (level)
  no operation moved by 1% of the time
where the time goes in v1:
time: 340 us; the launch traced here: 339 us
  waiting for transfers between devices  220 us (65%)
  matrix products  67.4 us (20%)
  blocking collectives  17.3 us (5%)
  other arithmetic  16.9 us (5%)
  between operations  14 us (4%)
    reduce_scatter x1, waiting for transfers between devices, shards(): lax.psum_scatter(jnp.dot(attended, w_out, preferred_element_type=jnp.floa...  54.9 us
    all_gather x1, waiting for transfers between devices, shards(): lax.all_gather(normed, 'tensor', axis=0, tiled=True)  54.5 us
    reduce_scatter x1, waiting for transfers between devices, shards(): lax.psum_scatter(placed.astype(jnp.bfloat16), 'tensor', scatter_dimension...  53.1 us
    all_gather x1, waiting for transfers between devices, shards(): lax.all_gather(normed_ffn, 'tensor', axis=0, tiled=True)  40.4 us
    dot_general x1, matrix products, expert_apply(): output = jnp.dot(hidden_act, w_down, preferred_element_type=jnp.float32)  23.2 us
    all_gather x1, waiting for transfers between devices, shards(): lax.all_gather(kv_rows, 'seq', axis=0, tiled=True)  17.4 us
    dot_general x1, matrix products, expert_apply(): lax.dot_general(slot_rows, w_gate_up[0], contract, preferred_element_type...  12.5 us
    all_gather x1, blocking collectives, shards(): lax.all_gather(expert_ids, 'tensor', axis=0, tiled=True)  9.15 us
  transfers between devices with their start and end apart: 5, of which 5 were waited for; matrix products, arithmetic and copies ran while one was open for 0% of the time, Pallas kernels for 0%

profile of v1, /device:TPU:0, one launch (start us, length us, event | category | flops | bytes accessed | tf_op | source)
XLA Modules:
  0.0 339.1 jit_solution(13860457289444476095)
XLA Ops:
  7.2 1.3 fusion.20
  8.6 2.1 fusion.22
  10.8 54.5 %all-gather.4.cloned.1.call-done = bf16[1024,2304]{1,0:T(8,128)(2,1)} async-done(((bf16[128,2304]{1,0:T(8,128)(2,1)}), bf16[1024,2304]{1,0:T(8,128)(2,1)}) %all-gather.4.cloned.1.call-update) | async-done | bytes 4718608 | tf_op jit(solution)/shard_map/all_gather | solution.py:121
  65.3 4.0 %fusion.95 = f32[1024,192]{0,1:S(1)} fusion(bf16[1024,2304]{1,0:T(8,128)(2,1)} %all-gather.4.cloned.1.call-done, bf16[2304,192]{0,1:T(8,128)(2,1)S(1)} %bitcast.62), kind=kOutput, calls=%fused_computation.120 | convolution fusion | flops 905969664 | bytes 6389760
  70.7 8.1 %all_gather.15 = s32[4096]{0:T(1024)S(1)} all-gather(s32[1024]{0:T(1024)S(1)} %copy-done.8), channel_id=1, replica_groups=mesh['seq'=4,'tensor'=8] {'seq'}, dimensions={0}, use_global_device_ids=true | all-gather | bytes 20480 | tf_op jit(solution)/shard_map/all_gather | solution.py:146
  78.9 17.4 %all-gather.6.cloned.1.call-done = bf16[4096,1,128]{0,2,1:T(8,128)(2,1)} async-done(((bf16[1024,1,128]{0,2,1:T(8,128)(2,1)}), bf16[4096,1,128]{0,2,1:T(8,128)(2,1)}) %all-gather.6.cloned.1.call-update) | async-done | bytes 1048592 | tf_op jit(solution)/shard_map/all_gather | solution.py:145
  96.3 2.3 fusion.41
  98.6 4.1 %fusion.8 = (f32[1024]{0:T(1024)S(1)}, f32[1024]{0:T(1024)S(1)}, f32[1024,2048]{1,0:T(8,128)S(1)}) fusion(s32[2048]{0:T(1024)S(1)} %iota_add_fusion, s32[2048]{0:T(1024)S(1)} %get-tuple-element.23, s32[1024]{0:T(1024)S(1)} %iota_add_fusion.1, s32[1024]{0:T(1024)S(1)} %copy-done.8, f32[1024,2048]{1,0:T(8,128)S(1)} %fusion.41, ...), kind=kOutput, calls=%fused_computation.14 | convolution fusion | flops 293861376 | bytes 17211392 | tf_op jit(solution)/shard_map/qhd,khd->hqk/dot_general | solution.py:49
  102.7 6.2 %fusion.12 = (f32[1024]{0:T(1024)S(1)}, f32[1024]{0:T(1024)S(1)}) fusion(f32[1024,2048]{1,0:T(8,128)S(1)} %fusion.41, f32[1024]{0:T(1024)S(1)} %get-tuple-element.26, s32[2048]{0:T(1024)S(1)} %get-tuple-element.22, s32[1024]{0:T(1024)S(1)} %iota_add_fusion.1, s32[1024]{0:T(1024)S(1)} %copy-done.8, f32[1024]{0:T(1024)S(1)} %get-tuple-element.25, ...), kind=kLoop, calls=%fused_computation.21 | loop fusion | flops 33552384 | bytes 16826368 | tf_op jit(solution)/shard_map/reduce_sum | solution.py:59
  108.9 2.8 fusion.29
  111.7 8.0 %convolution_convert_fusion.1 = bf16[1024,2304]{1,0:T(8,128)(2,1)} fusion(bf16[64,2304]{1,0:T(8,128)(2,1)S(1)} %copy-done.11, f32[1024,64]{0,1:T(8,128)S(1)} %fusion.29, f32[1024,2048]{1,0:T(8,128)} %copy-done.4, f32[1024]{0:T(1024)S(1)} %get-tuple-element.25, s32[2048]{0:T(1024)S(1)} %iota_add_fusion, s32[2048]{0:T(1024)S(1)} %get-tuple-element.23, ...), kind=kOutput, calls=%fused_computation.17 | convolution fusion | flops 589758464 | bytes 13959168 | tf_op jit(solution)/shard_map/dot_general | solution.py:157
  120.0 54.9 %reduce-scatter.3.cloned.1.call-done = bf16[128,2304]{1,0:T(8,128)(2,1)} async-done(((bf16[1024,2304]{1,0:T(8,128)(2,1)}), bf16[128,2304]{1,0:T(8,128)(2,1)}) %reduce-scatter.3.cloned.1.call-update) | async-done | bytes 589840 | tf_op jit(solution)/shard_map/reduce_scatter | solution.py:156
  174.9 1.3 multiply_reduce_fusion
  176.2 2.1 multiply_convert_fusion.1
  178.4 9.2 %all_gather.18 = s32[1024,2]{0,1:T(2,128)S(1)} all-gather(s32[128,2]{0,1:T(2,128)S(1)} %copy-done.10), channel_id=1, replica_groups=mesh['seq'=4,'tensor'=8] {'tensor'}, dimensions={0}, use_global_device_ids=true | all-gather | bytes 9216 | tf_op jit(solution)/shard_map/all_gather | solution.py:170
  188.1 40.4 %all-gather.8.cloned.1.call-done = bf16[1024,2304]{1,0:T(8,128)(2,1)} async-done(((bf16[128,2304]{1,0:T(8,128)(2,1)}), bf16[1024,2304]{1,0:T(8,128)(2,1)}) %all-gather.8.cloned.1.call-update) | async-done | bytes 4718608 | tf_op jit(solution)/shard_map/all_gather | solution.py:169
  228.6 3.1 convolution_convert_fusion.2
  231.7 1.5 copy-done.3
  233.2 1.9 fusion.96
  235.3 12.5 %fusion.2 = f32[512,2880]{0,1:T(8,128)} fusion(bf16[512,2304]{1,0:T(8,128)(2,1)} %bitcast.65, bf16[2,2880,2304]{2,1,0:T(8,128)(2,1)} %param.16), kind=kOutput, calls=%fused_computation.2 | convolution fusion | flops 6794772480 | bytes 21528576 | tf_op jit(solution)/shard_map/dot_general | solution.py:90
  248.0 23.2 %fusion.11 = bf16[512,2304]{1,0:T(8,128)(2,1)} fusion(bf16[2880,2304]{1,0:T(8,128)(2,1)} %param.17, f32[512]{0:T(512)S(1)} %mul.193, f32[512,2880]{0,1:T(8,128)} %fusion.2, bf16[512,2304]{1,0:T(8,128)(2,1)} %bitcast.66, bf16[2,2880,2304]{2,1,0:T(8,128)(2,1)} %param.16), kind=kOutput, calls=%fused_computation.20 | convolution fusion | flops 13600751616 | bytes 37160960 | tf_op jit(solution)/shard_map/dot_general | solution.py:95
  271.2 5.3 %convolution_convert_fusion = bf16[8,128,2304]{2,1,0:T(8,128)(2,1)} fusion(bf16[8,64,2304]{2,1,0:T(8,128)(2,1)} %bitcast.68, s32[8,128]{1,0:T(8,128)S(1)} %broadcast_add_fusion, pred[8,128]{1,0:T(8,128)(4,1)S(1)} %broadcast_compare_fusion), kind=kOutput, calls=%fused_computation.16 | convolution fusion | flops 304480256 | bytes 7083008 | tf_op jit(solution)/shard_map/sjr,sjd->srd/dot_general | solution.py:193
  277.4 53.1 %reduce-scatter.5.cloned.1.call-done = bf16[128,2304]{1,0:T(8,128)(2,1)} async-done(((bf16[1024,2304]{1,0:T(8,128)(2,1)}), bf16[128,2304]{1,0:T(8,128)(2,1)}) %reduce-scatter.5.cloned.1.call-update) | async-done | bytes 589840 | tf_op jit(solution)/shard_map/reduce_scatter | solution.py:199
  330.5 2.1 add_convert_fusion
  (63 shorter events, 3.8 us)
Async XLA Ops:
  7.2 58.1 %copy-start = (bf16[3,2304,64]{1,2,0:T(8,128)(2,1)S(1)}, bf16[3,2304,64]{1,2,0:T(8,128)(2,1)}, u32[]{:S(2)}) copy-start(bf16[3,2304,64]{1,2,0:T(8,128)(2,1)} %param.13) | copy-start | bytes 2654212
  7.2 63.5 %copy-start.8 = (s32[1024]{0:T(1024)S(1)}, s32[1024]{0:T(1024)}, u32[]{:S(2)}) copy-start(s32[1024]{0:T(1024)} %param.18) | copy-start | bytes 12292
  7.2 58.1 %all-gather.4.cloned.1.call-start = ((), (), s32[]{:S(2)}) async-start(), calls=%async_computation.2 | async-start | bytes 5308416 | tf_op jit(solution)/shard_map/all_gather | solution.py:121
  10.7 85.6 %all-gather.6.cloned.1.call-start = ((), (), s32[]{:S(2)}) async-start(), calls=%async_computation.3 | async-start | bytes 1310720 | tf_op jit(solution)/shard_map/all_gather | solution.py:145
  70.7 104.2 %reduce-scatter.3.cloned.1.call-start = ((), (), s32[]{:S(2)}) async-start(), calls=%async_computation.4 | async-start | bytes 5308416 | tf_op jit(solution)/shard_map/reduce_scatter | solution.py:156
  96.3 2.3 copy-start.7
  102.7 6.2 %copy-start.4 = (f32[1024,2048]{1,0:T(8,128)}, f32[1024,2048]{1,0:T(8,128)S(1)}, u32[]{:S(2)}) copy-start(f32[1024,2048]{1,0:T(8,128)S(1)} %get-tuple-element.27) | copy-start | bytes 25165828
  108.9 2.8 copy-start.11
  111.7 63.2 %copy-start.2 = (bf16[128,2304]{1,0:T(8,128)(2,1)S(1)}, bf16[128,2304]{1,0:T(8,128)(2,1)}, u32[]{:S(2)}) copy-start(bf16[128,2304]{1,0:T(8,128)(2,1)} %param.10) | copy-start | bytes 1769476
  119.7 56.5 %copy-start.9 = (f32[2304]{0:T(1024)S(1)}, f32[2304]{0:T(1024)}, u32[]{:S(2)}) copy-start(f32[2304]{0:T(1024)} %param.12) | copy-start | bytes 27652
  119.7 58.7 %copy-start.10 = (s32[128,2]{0,1:T(2,128)S(1)}, s32[128,2]{0,1:T(2,128)}, u32[]{:S(2)}) copy-start(s32[128,2]{0,1:T(2,128)} %param.19) | copy-start | bytes 3076
  119.8 113.4 %copy-start.6 = (f32[2304,8]{0,1:T(8,128)S(1)}, f32[2304,8]{0,1:T(8,128)}, u32[]{:S(2)}) copy-start(f32[2304,8]{0,1:T(8,128)} %param.15) | copy-start | bytes 221188
  119.8 108.8 %all-gather.8.cloned.1.call-start = ((), (), s32[]{:S(2)}) async-start(), calls=%async_computation.5 | async-start | bytes 5308416 | tf_op jit(solution)/shard_map/all_gather | solution.py:169
  178.4 152.1 %reduce-scatter.5.cloned.1.call-start = ((), (), s32[]{:S(2)}) async-start(), calls=%async_computation.6 | async-start | bytes 5308416 | tf_op jit(solution)/shard_map/reduce_scatter | solution.py:199
  231.7 1.5 copy-start.3
  271.2 61.4 %copy-start.1 = (bf16[3,2304,64]{1,2,0:T(8,128)(2,1)S(1)}, bf16[3,2304,64]{1,2,0:T(8,128)(2,1)}, u32[]{:S(2)}) copy-start(bf16[3,2304,64]{1,2,0:T(8,128)(2,1)} %param.13) | copy-start | bytes 2654212
  271.2 59.3 %copy-start.5 = (bf16[128,2304]{1,0:T(8,128)(2,1)S(1)}, bf16[128,2304]{1,0:T(8,128)(2,1)}, u32[]{:S(2)}) copy-start(bf16[128,2304]{1,0:T(8,128)(2,1)} %reduce-scatter.3.cloned.1.call-done) | copy-start | bytes 1769476
Sparse Core Ops, SparseCore 0:
  10.8 54.3 all-gather.3
  70.8 25.4 all-gather.5
  119.9 54.9 reduce-scatter.2
  178.5 50.0 all-gather.7
  276.7 53.7 reduce-scatter.4

commit v2 on v1

--- a/solution.py
+++ b/solution.py
@@ -57,14 +57,24 @@
         weights = jnp.where(allowed[None], jnp.exp(masked - new_max[..., None]), 0.0)
         factor = jnp.exp(running_max - new_max)
         denominator = denominator * factor + jnp.sum(weights, axis=-1)
-        weighted_sum = weighted_sum * factor[..., None] + jnp.einsum(
-            "hqk,khd->hqd",
+        weighted_sum = weighted_sum * factor[:, None, :] + jnp.einsum(
+            "hqk,khd->hdq",
             weights.astype(jnp.bfloat16),
             value_block,
             preferred_element_type=jnp.float32,
         )
         running_max = new_max
     return (running_max, denominator, weighted_sum)
+
+
+def pack_ids(ids, width):
+    flat = ids.reshape(-1).astype(jnp.bfloat16)
+    row_count = -(-flat.shape[0] // (16 * width)) * 16
+    return jnp.pad(flat, (0, row_count * width - flat.shape[0])).reshape(row_count, width)
+
+
+def unpack_ids(packed, count):
+    return packed.reshape(packed.shape[0], -1)[:, :count].astype(jnp.int32)
 
 
 def slot_table(token_ids, target, slot_count):
@@ -115,10 +125,10 @@
     seq_place = lax.axis_index("seq")
     group_rows = local_rows * tensor_count
     head_count = w_qkv.shape[2] // HD
-    normed = rms_norm(hidden_in, norm_attn)
+    full_hidden = lax.all_gather(hidden_in, "tensor", axis=0, tiled=True)
     projected = jnp.einsum(
         "td,cdh->tch",
-        lax.all_gather(normed, "tensor", axis=0, tiled=True),
+        rms_norm(full_hidden, norm_attn),
         w_qkv,
         preferred_element_type=jnp.float32,
     )
@@ -132,43 +142,49 @@
     value_rows = projected[:, 2].reshape(group_rows, head_count, HD).astype(jnp.bfloat16)
     kv_rows = jnp.concatenate([key_rows, value_rows], axis=-1)
     kv_cache = kv_rows.transpose(1, 0, 2)
+    seq_count = lax.axis_size("seq")
+    kv_flat = kv_cache.reshape(head_count * group_rows, 2 * HD)
+    kv_packed = jnp.concatenate([kv_flat, pack_ids(segment_ids, 2 * HD)], axis=0)
+    out_packed = jnp.concatenate([w_out, pack_ids(expert_ids, model_width)], axis=0)
+    kv_packed, out_packed = lax.optimization_barrier((kv_packed, out_packed))
+    kv_gathered = lax.all_gather(kv_packed, "seq", axis=0)
+    out_gathered = lax.all_gather(out_packed, "tensor", axis=0)
+    all_segments = unpack_ids(kv_gathered[:, kv_flat.shape[0] :], group_rows).reshape(-1)
+    all_kv = (
+        kv_gathered[:, : kv_flat.shape[0]]
+        .reshape(seq_count, head_count, group_rows, 2 * HD)
+        .transpose(0, 2, 1, 3)
+        .reshape(seq_count * group_rows, head_count, 2 * HD)
+    )
+    full_ids = unpack_ids(out_gathered[:, w_out.shape[0] :], 2 * local_rows)
+    w_out_full = out_gathered[:, : w_out.shape[0]].reshape(-1, model_width)
     start_state = (
         jnp.full((head_count, group_rows), low_score, jnp.float32),
         jnp.zeros((head_count, group_rows), jnp.float32),
-        jnp.zeros((head_count, group_rows, HD), jnp.float32),
+        jnp.zeros((head_count, HD, group_rows), jnp.float32),
     )
     softmax_state = fold_keys(
-        start_state,
-        query_rows,
-        segment_ids,
-        positions,
-        lax.all_gather(kv_rows, "seq", axis=0, tiled=True),
-        lax.all_gather(segment_ids, "seq", axis=0, tiled=True),
-        jnp.int32(0),
+        start_state, query_rows, segment_ids, positions, all_kv, all_segments, jnp.int32(0)
     )
     running_max, denominator, weighted_sum = softmax_state
     attended = (
-        (weighted_sum / denominator[..., None])
-        .transpose(1, 0, 2)
-        .reshape(group_rows, head_count * HD)
+        (weighted_sum / denominator[:, None, :])
         .astype(jnp.bfloat16)
-    )
-    attention_sum = lax.psum_scatter(
-        jnp.dot(attended, w_out, preferred_element_type=jnp.float32).astype(jnp.bfloat16),
-        "tensor",
-        scatter_dimension=0,
-        tiled=True,
-    ).astype(jnp.float32)
-    residual = hidden_in.astype(jnp.float32) + attention_sum
-    normed_ffn = rms_norm(residual, norm_ffn)
+        .reshape(head_count * HD, group_rows)
+    )
+    attention_sum = lax.dot_general(
+        lax.all_gather(attended, "tensor", axis=0, tiled=True),
+        w_out_full,
+        (((0,), (0,)), ((), ())),
+        preferred_element_type=jnp.float32,
+    )
+    full_residual = full_hidden.astype(jnp.float32) + attention_sum
+    full_rows = rms_norm(full_residual, norm_ffn)
+    residual = lax.dynamic_slice_in_dim(full_residual, tensor_place * local_rows, local_rows, 0)
     expert_count = w_router.shape[1]
     slice_count = tensor_count // expert_count
     own_expert = tensor_place // slice_count
     slot_count = local_rows // 2
-    full_rows, full_ids = (
-        lax.all_gather(normed_ffn, "tensor", axis=0, tiled=True),
-        lax.all_gather(expert_ids, "tensor", axis=0, tiled=True),
-    )
     block_ids = full_ids.reshape(tensor_count, local_rows, 2)
     slot_tables = jax.vmap(lambda source_ids: slot_table(source_ids, own_expert, slot_count))(
         block_ids

time: 340 us -> 291 us (0.86)
  waiting for transfers between devices: 220 us -> 170 us
  blocking collectives: 17.3 us -> 0 us
  local copies, waits for them, and re-layouts: 2.76 us -> 14.5 us
  other arithmetic: 16.9 us -> 22.9 us
    reduce_scatter x1 -> x0, waiting for transfers between devices: 54.9 us -> none  [shards(): lax.psum_scatter(jnp.dot(attended, w_out, preferred_element_type=jnp.floa...]
    all_gather x2 -> x0, blocking collectives: 17.3 us -> none  [the longest x1 9.15 us: shards(): lax.all_gather(expert_ids, 'tensor', axis=0, tiled=True)]
    slice x1 -> x4, local copies, waits for them, and re-layouts: 0.01 us -> 10.9 us  [the longest x2 7.75 us: shards(): full_ids = unpack_ids(out_gathered[:, w_out.shape[0]:], 2 * local_rows)]
    dot_general x2 -> x3, matrix products: 10.8 us -> 16.1 us  [the longest x1 9.31 us: shards(): lax.dot_general(lax.all_gather(attended, 'tensor', axis=0, tiled=True), w...]
    all_gather x3 -> x4, waiting for transfers between devices: 112 us -> 115 us  [the longest x1 52.4 us: shards(): full_hidden = lax.all_gather(hidden_in, 'tensor', axis=0, tiled=True)]
  transfers between devices with their start and end apart: 5 -> 5, of which waited for: 5 -> 5; matrix products, arithmetic and copies ran while one was open for 0% -> 10% of each run, Pallas kernels for 0% -> 0%
where the time goes in v2:
time: 291 us; the launch traced here: 290 us
  waiting for transfers between devices  170 us (58%)
  matrix products  68.3 us (23%)
  other arithmetic  22.9 us (8%)
  local copies, waits for them, and re-layouts  14.5 us (5%)
  between operations  14.1 us (5%)
    reduce_scatter x1, waiting for transfers between devices, shards(): lax.psum_scatter(placed.astype(jnp.bfloat16), 'tensor', scatter_dimension...  53.9 us
    all_gather x1, waiting for transfers between devices, shards(): full_hidden = lax.all_gather(hidden_in, 'tensor', axis=0, tiled=True)  52.4 us
    all_gather x1, waiting for transfers between devices, shards(): kv_gathered = lax.all_gather(kv_packed, 'seq', axis=0)  25 us
    dot_general x1, matrix products, expert_apply(): output = jnp.dot(hidden_act, w_down, preferred_element_type=jnp.float32)  22 us
    all_gather x1, waiting for transfers between devices, shards(): lax.all_gather(attended, 'tensor', axis=0, tiled=True)  20.1 us
    all_gather x1, waiting for transfers between devices, shards(): out_gathered = lax.all_gather(out_packed, 'tensor', axis=0)  17.4 us
    dot_general x1, matrix products, expert_apply(): lax.dot_general(slot_rows, w_gate_up[0], contract, preferred_element_type...  11.8 us
    dot_general x1, matrix products, shards(): lax.dot_general(lax.all_gather(attended, 'tensor', axis=0, tiled=True), w...  9.31 us
  transfers between devices with their start and end apart: 5, of which 5 were waited for; matrix products, arithmetic and copies ran while one was open for 10% of the time, Pallas kernels for 0%

profile of v2, /device:TPU:0, one launch (start us, length us, event | category | flops | bytes accessed | tf_op | source)
XLA Modules:
  0.0 290.1 jit_solution(12086984493946655044)
XLA Ops:
  9.9 1.7 pad_maximum_fusion
  11.7 52.4 %all-gather.7.cloned.1.call-done = bf16[1024,2304]{1,0:T(8,128)(2,1)} async-done(((bf16[128,2304]{1,0:T(8,128)(2,1)}), bf16[1024,2304]{1,0:T(8,128)(2,1)}) %all-gather.7.cloned.1.call-update) | async-done | bytes 4718608 | tf_op jit(solution)/shard_map/all_gather | solution.py:128
  64.1 3.3 %fusion.6 = f32[1024]{0:T(1024)S(1)} fusion(bf16[1024,2304]{1,0:T(8,128)(2,1)} %all-gather.7.cloned.1.call-done), kind=kLoop, calls=%fused_computation.9 | loop fusion | flops 7076864 | bytes 4722688 | tf_op jit(solution)/shard_map/reduce_sum | solution.py:17
  67.4 4.1 %fusion.14 = f32[1024,192]{0,1:S(1)} fusion(bf16[2304,192]{0,1:T(8,128)(2,1)S(1)} %bitcast.79, bf16[1024,2304]{1,0:T(8,128)(2,1)} %all-gather.7.cloned.1.call-done, f32[2304]{0:T(1024)} %param.11, f32[1024]{0:T(1024)S(1)} %add_rsqrt_fusion.1), kind=kOutput, calls=%fused_computation.26 | convolution fusion | flops 915406848 | bytes 6403072
  74.0 25.0 %all-gather.11.cloned.1.call-done = bf16[4160,128]{1,0:T(8,128)(2,1)} async-done(((bf16[1040,128]{1,0:T(8,128)(2,1)}), bf16[4160,128]{1,0:T(8,128)(2,1)}) %all-gather.11.cloned.1.call-update) | async-done | bytes 1064976 | tf_op jit(solution)/shard_map/all_gather | solution.py:150
  99.6 1.3 fusion.91
  101.0 1.3 fusion.43
  102.3 4.7 %fusion.11 = (f32[1024]{0:T(1024)S(1)}, f32[1024]{0:T(1024)S(1)}, f32[1024,2048]{1,0:T(8,128)S(1)}) fusion(s32[2048]{0:T(1024)S(1)} %iota_add_fusion, s32[2048]{0:T(1024)S(1)} %get-tuple-element.42, s32[1024]{0:T(1024)S(1)} %iota_add_fusion.1, s32[1024]{0:T(1024)S(1)} %copy-done.3, f32[1024,2048]{1,0:T(8,128)S(1)} %fusion.43, ...), kind=kOutput, calls=%fused_computation.22 | convolution fusion | flops 293861376 | bytes 17473536 | tf_op jit(solution)/shard_map/qhd,khd->hqk/dot_general | solution.py:49
  107.0 6.5 %fusion.19 = (f32[1024]{0:T(1024)S(1)}, f32[1024]{0:T(1024)S(1)}) fusion(f32[1024,2048]{1,0:T(8,128)S(1)} %fusion.43, f32[1024]{0:T(1024)S(1)} %get-tuple-element.34, s32[2048]{0:T(1024)S(1)} %get-tuple-element.43, s32[1024]{0:T(1024)S(1)} %iota_add_fusion.1, s32[1024]{0:T(1024)S(1)} %copy-done.3, f32[1024]{0:T(1024)S(1)} %get-tuple-element.33, ...), kind=kLoop, calls=%fused_computation.31 | loop fusion | flops 33552384 | bytes 16826368 | tf_op jit(solution)/shard_map/reduce_sum | solution.py:59
  113.5 3.2 %fusion.33 = f32[64,1024]{1,0:T(8,128)S(1)} fusion(f32[1024,2048]{1,0:T(8,128)S(1)} %fusion.43, f32[1024]{0:T(1024)S(1)} %get-tuple-element.34, s32[2048]{0:T(1024)S(1)} %get-tuple-element.43, s32[1024]{0:T(1024)S(1)} %iota_add_fusion.1, s32[1024]{0:T(1024)S(1)} %copy-done.3, bf16[2048,1,128]{2,0,1:T(8,128)(2,1)S(1)} %bitcast.92, ...), kind=kOutput, calls=%fused_computation.40 | convolution fusion | flops 285343744 | bytes 9203712 | tf_op jit(solution)/shard_map/hqk,khd->hdq/dot_general | solution.py:60
  116.7 3.6 %fusion.39 = bf16[64,1024]{1,0:T(8,128)(2,1)} fusion(f32[64,1024]{1,0:T(8,128)S(1)} %fusion.33, f32[1024,2048]{1,0:T(8,128)S(1)} %get-tuple-element.37, f32[1024]{0:T(1024)S(1)} %get-tuple-element.33, s32[2048]{0:T(1024)S(1)} %iota_add_fusion, s32[2048]{0:T(1024)S(1)} %get-tuple-element.42, s32[1024]{0:T(1024)S(1)} %iota_add_fusion.1, ...), kind=kOutput, calls=%fused_computation.43 | convolution fusion | flops 285409280 | bytes 9338880 | tf_op jit(solution)/shard_map/hqk,khd->hdq/dot_general | solution.py:60
  120.4 17.4 %all-gather.13.cloned.1.call-done = bf16[640,2304]{1,0:T(8,128)(2,1)} async-done(((bf16[80,2304]{1,0:T(8,128)(2,1)}), bf16[640,2304]{1,0:T(8,128)(2,1)}) %all-gather.13.cloned.1.call-update) | async-done | bytes 2949136 | tf_op jit(solution)/shard_map/all_gather | solution.py:151
  137.8 1.1 slice.116
  139.0 1.8 slice.115
  140.8 20.1 %all-gather.9.cloned.1.call-done = bf16[512,1024]{1,0:T(8,128)(2,1)} async-done(((bf16[64,1024]{1,0:T(8,128)(2,1)}), bf16[512,1024]{1,0:T(8,128)(2,1)}) %all-gather.9.cloned.1.call-update) | async-done | bytes 1048592 | tf_op jit(solution)/shard_map/all_gather | solution.py:176
  160.9 9.3 %multiply_reduce_fusion = (f32[1024]{0:T(1024)S(1)}, f32[1024,2304]{1,0:T(8,128)}) fusion(bf16[512,1024]{1,0:T(8,128)(2,1)} %all-gather.9.cloned.1.call-done, bf16[512,2304]{1,0:T(8,128)(2,1)S(1)} %bitcast.90, bf16[1024,2304]{1,0:T(8,128)(2,1)} %all-gather.7.cloned.1.call-done), kind=kOutput, calls=%fused_computation.13 | convolution fusion | flops 2425355264 | bytes 17567744 | tf_op jit(solution)/shard_map/dot_general | solution.py:175
  170.2 6.6 %copy.49 = bf16[8,16,2304]{0,2,1:T(8,128)(2,1)} copy(bf16[8,16,2304]{2,1,0:T(8,128)(2,1)S(1)} %slice.116) | data formatting | bytes 1179648 | tf_op jit(solution)/shard_map/slice | solution.py:159
  179.3 4.6 %multiply_convert_fusion = bf16[1024,2304]{1,0:T(8,128)(2,1)S(1)} fusion(f32[1024,2304]{1,0:T(8,128)} %get-tuple-element.39, f32[2304]{0:T(1024)S(1)} %copy-done.4, f32[1024]{0:T(1024)S(1)} %add_rsqrt_fusion), kind=kLoop, calls=%fused_computation.12 | loop fusion | flops 7077888 | bytes 14169088 | tf_op jit(solution)/shard_map/convert_element_type | solution.py:18
  184.9 1.9 fusion.92
  187.3 11.8 %fusion.2 = f32[512,2880]{0,1:T(8,128)} fusion(bf16[512,2304]{1,0:T(8,128)(2,1)S(1)} %bitcast.85, bf16[2,2880,2304]{2,1,0:T(8,128)(2,1)} %param.16), kind=kOutput, calls=%fused_computation.5 | convolution fusion | flops 6794772480 | bytes 21528576 | tf_op jit(solution)/shard_map/dot_general | solution.py:100
  199.1 22.0 %fusion.18 = bf16[512,2304]{1,0:T(8,128)(2,1)} fusion(bf16[2880,2304]{1,0:T(8,128)(2,1)} %param.17, f32[512]{0:T(512)S(1)} %mul.197, f32[512,2880]{0,1:T(8,128)} %fusion.2, bf16[512,2304]{1,0:T(8,128)(2,1)S(1)} %bitcast.86, bf16[2,2880,2304]{2,1,0:T(8,128)(2,1)} %param.16), kind=kOutput, calls=%fused_computation.30 | convolution fusion | flops 13600751616 | bytes 37160960 | tf_op jit(solution)/shard_map/dot_general | solution.py:105
  221.1 5.3 %convolution_convert_fusion = bf16[8,128,2304]{2,1,0:T(8,128)(2,1)} fusion(bf16[8,64,2304]{2,1,0:T(8,128)(2,1)} %bitcast.89, s32[8,128]{1,0:T(8,128)S(1)} %broadcast_add_fusion, pred[8,128]{1,0:T(8,128)(4,1)S(1)} %get-tuple-element.35), kind=kOutput, calls=%fused_computation.24 | convolution fusion | flops 304480256 | bytes 7083008 | tf_op jit(solution)/shard_map/sjr,sjd->srd/dot_general | solution.py:209
  227.3 53.9 %reduce-scatter.2.cloned.1.call-done = bf16[128,2304]{1,0:T(8,128)(2,1)} async-done(((bf16[1024,2304]{1,0:T(8,128)(2,1)}), bf16[128,2304]{1,0:T(8,128)(2,1)}) %reduce-scatter.2.cloned.1.call-update) | async-done | bytes 589840 | tf_op jit(solution)/shard_map/reduce_scatter | solution.py:215
  281.2 2.4 add_convert_fusion
  (69 shorter events, 10.6 us)
Async XLA Ops:
  7.2 60.3 %copy-start = (bf16[3,2304,64]{1,2,0:T(8,128)(2,1)S(1)}, bf16[3,2304,64]{1,2,0:T(8,128)(2,1)}, u32[]{:S(2)}) copy-start(bf16[3,2304,64]{1,2,0:T(8,128)(2,1)} %param.13) | copy-start | bytes 2654212
  7.2 56.9 %all-gather.7.cloned.1.call-start = ((), (), s32[]{:S(2)}) async-start(), calls=%async_computation.1 | async-start | bytes 5308416 | tf_op jit(solution)/shard_map/all_gather | solution.py:128
  7.9 91.0 %all-gather.11.cloned.1.call-start = ((), (), s32[]{:S(2)}) async-start(), calls=%async_computation.4 | async-start | bytes 1331200 | tf_op jit(solution)/shard_map/all_gather | solution.py:150
  72.3 30.0 %copy-start.3 = (s32[1024]{0:T(1024)S(1)}, s32[1024]{0:T(1024)}, u32[]{:S(2)}) copy-start(s32[1024]{0:T(1024)} %param.18) | copy-start | bytes 12292
  73.2 64.7 %all-gather.13.cloned.1.call-start = ((), (), s32[]{:S(2)}) async-start(), calls=%async_computation.5 | async-start | bytes 3317760 | tf_op jit(solution)/shard_map/all_gather | solution.py:151
  73.9 87.0 %all-gather.9.cloned.1.call-start = ((), (), s32[]{:S(2)}) async-start(), calls=%async_computation.2 | async-start | bytes 1179648 | tf_op jit(solution)/shard_map/all_gather | solution.py:176
  120.4 160.8 %reduce-scatter.2.cloned.1.call-start = ((), (), s32[]{:S(2)}) async-start(), calls=%async_computation.3 | async-start | bytes 5308416 | tf_op jit(solution)/shard_map/reduce_scatter | solution.py:215
  170.2 9.1 %copy-start.4 = (f32[2304]{0:T(1024)S(1)}, f32[2304]{0:T(1024)}, u32[]{:S(2)}) copy-start(f32[2304]{0:T(1024)} %param.12) | copy-start | bytes 27652
  179.3 5.7 %copy-start.2 = (f32[2304,8]{0,1:T(8,128)S(1)}, f32[2304,8]{0,1:T(8,128)}, u32[]{:S(2)}) copy-start(f32[2304,8]{0,1:T(8,128)} %param.15) | copy-start | bytes 221188
  199.1 84.5 %copy-start.1 = (bf16[3,2304,64]{1,2,0:T(8,128)(2,1)S(1)}, bf16[3,2304,64]{1,2,0:T(8,128)(2,1)}, u32[]{:S(2)}) copy-start(bf16[3,2304,64]{1,2,0:T(8,128)(2,1)} %param.13) | copy-start | bytes 2654212
Sparse Core Ops, SparseCore 0:
  9.7 54.3 all-gather.6
  73.3 25.5 all-gather.10
  101.1 36.6 all-gather.12
  139.9 20.9 all-gather.8
  226.6 54.5 reduce-scatter.1

commit v3 on v2

--- a/solution.py
+++ b/solution.py
@@ -172,6 +172,7 @@
         .astype(jnp.bfloat16)
         .reshape(head_count * HD, group_rows)
     )
+    attended, w_out_full = lax.optimization_barrier((attended, w_out_full))
     attention_sum = lax.dot_general(
         lax.all_gather(attended, "tensor", axis=0, tiled=True),
         w_out_full,

time: 291 us -> 276 us (0.948)
  waiting for transfers between devices: 170 us -> 161 us
  other arithmetic: 22.9 us -> 19.2 us
  matrix products: 68.3 us -> 65.1 us
    all_gather x1, waiting for transfers between devices: 20.1 us -> 10.6 us  [shards(): lax.all_gather(attended, 'tensor', axis=0, tiled=True)]
    convert_element_type x1, other arithmetic: 4.6 us -> 0.9 us  [rms_norm(): return (as_float * scale * gain).astype(jnp.bfloat16)]
    dot_general x1, matrix products: 9.31 us -> 6.07 us  [shards(): lax.dot_general(lax.all_gather(attended, 'tensor', axis=0, tiled=True), w...]
  transfers between devices with their start and end apart: 5 -> 5, of which waited for: 5 -> 5; matrix products, arithmetic and copies ran while one was open for 10% -> 13% of each run, Pallas kernels for 0% -> 0%
where the time goes in v3:
time: 276 us
  waiting for transfers between devices  161 us (58%)
  matrix products  65.1 us (24%)
  other arithmetic  19.2 us (7%)
  local copies, waits for them, and re-layouts  16.4 us (6%)
  between operations  14.1 us (5%)
    reduce_scatter x1, waiting for transfers between devices, shards(): lax.psum_scatter(placed.astype(jnp.bfloat16), 'tensor', scatter_dimension...  53.9 us
    all_gather x1, waiting for transfers between devices, shards(): full_hidden = lax.all_gather(hidden_in, 'tensor', axis=0, tiled=True)  52.4 us
    all_gather x1, waiting for transfers between devices, shards(): kv_gathered = lax.all_gather(kv_packed, 'seq', axis=0)  25 us
    dot_general x1, matrix products, expert_apply(): output = jnp.dot(hidden_act, w_down, preferred_element_type=jnp.float32)  22 us
    all_gather x1, waiting for transfers between devices, shards(): out_gathered = lax.all_gather(out_packed, 'tensor', axis=0)  17.5 us
    dot_general x1, matrix products, expert_apply(): lax.dot_general(slot_rows, w_gate_up[0], contract, preferred_element_type...  11.8 us
    all_gather x1, waiting for transfers between devices, shards(): lax.all_gather(attended, 'tensor', axis=0, tiled=True)  10.6 us
    slice x2, local copies, waits for them, and re-layouts, shards(): full_ids = unpack_ids(out_gathered[:, w_out.shape[0]:], 2 * local_rows)  7.77 us
  transfers between devices with their start and end apart: 5, of which 5 were waited for; matrix products, arithmetic and copies ran while one was open for 13% of the time, Pallas kernels for 0%

profile of v3, /device:TPU:0, one launch (start us, length us, event | category | flops | bytes accessed | tf_op | source)
XLA Modules:
  0.0 275.8 jit_solution(12241428553368744438)
XLA Ops:
  9.9 1.7 pad_maximum_fusion
  11.7 52.4 %all-gather.7.cloned.1.call-done = bf16[1024,2304]{1,0:T(8,128)(2,1)} async-done(((bf16[128,2304]{1,0:T(8,128)(2,1)}), bf16[1024,2304]{1,0:T(8,128)(2,1)}) %all-gather.7.cloned.1.call-update) | async-done | bytes 4718608 | tf_op jit(solution)/shard_map/all_gather | solution.py:128
  64.1 3.3 %fusion.6 = f32[1024]{0:T(1024)S(1)} fusion(bf16[1024,2304]{1,0:T(8,128)(2,1)} %all-gather.7.cloned.1.call-done), kind=kLoop, calls=%fused_computation.9 | loop fusion | flops 7076864 | bytes 4722688 | tf_op jit(solution)/shard_map/reduce_sum | solution.py:17
  67.4 4.1 %fusion.14 = f32[1024,192]{0,1:S(1)} fusion(bf16[2304,192]{0,1:T(8,128)(2,1)S(1)} %bitcast.81, bf16[1024,2304]{1,0:T(8,128)(2,1)} %all-gather.7.cloned.1.call-done, f32[2304]{0:T(1024)} %param.11, f32[1024]{0:T(1024)S(1)} %add_rsqrt_fusion.1), kind=kOutput, calls=%fused_computation.26 | convolution fusion | flops 915406848 | bytes 6403072
  74.0 25.0 %all-gather.11.cloned.1.call-done = bf16[4160,128]{1,0:T(8,128)(2,1)} async-done(((bf16[1040,128]{1,0:T(8,128)(2,1)}), bf16[4160,128]{1,0:T(8,128)(2,1)}) %all-gather.11.cloned.1.call-update) | async-done | bytes 1064976 | tf_op jit(solution)/shard_map/all_gather | solution.py:150
  99.6 1.3 fusion.91
  101.0 1.3 fusion.43
  102.3 4.7 %fusion.11 = (f32[1024]{0:T(1024)S(1)}, f32[1024]{0:T(1024)S(1)}, f32[1024,2048]{1,0:T(8,128)S(1)}) fusion(s32[2048]{0:T(1024)S(1)} %iota_add_fusion, s32[2048]{0:T(1024)S(1)} %bitcast.103, s32[1024]{0:T(1024)S(1)} %iota_add_fusion.1, s32[1024]{0:T(1024)S(1)} %copy-done.4, f32[1024,2048]{1,0:T(8,128)S(1)} %fusion.43, s32[2048]{0:T(1024)S(1)} %bitcast.106, ...), kind=kOutput, calls=%fused_computation.22 | convolution fusion | flops 293861376 | bytes 17473536 | tf_op jit(solution)/shard_map/qhd,khd->hqk/dot_general | solution.py:49
  107.0 6.5 %fusion.19 = (f32[1024]{0:T(1024)S(1)}, f32[1024]{0:T(1024)S(1)}) fusion(f32[1024,2048]{1,0:T(8,128)S(1)} %fusion.43, f32[1024]{0:T(1024)S(1)} %get-tuple-element.38, s32[2048]{0:T(1024)S(1)} %bitcast.107, s32[1024]{0:T(1024)S(1)} %iota_add_fusion.1, s32[1024]{0:T(1024)S(1)} %copy-done.4, f32[1024]{0:T(1024)S(1)} %get-tuple-element.37, ...), kind=kLoop, calls=%fused_computation.31 | loop fusion | flops 33552384 | bytes 16826368 | tf_op jit(solution)/shard_map/reduce_sum | solution.py:59
  113.5 3.2 %fusion.33 = f32[64,1024]{1,0:T(8,128)S(1)} fusion(f32[1024,2048]{1,0:T(8,128)S(1)} %fusion.43, f32[1024]{0:T(1024)S(1)} %get-tuple-element.38, s32[2048]{0:T(1024)S(1)} %bitcast.108, s32[1024]{0:T(1024)S(1)} %iota_add_fusion.1, s32[1024]{0:T(1024)S(1)} %copy-done.4, bf16[2048,1,128]{2,0,1:T(8,128)(2,1)S(1)} %bitcast.94, f32[1024]{0:T(1024)S(1)} %get-tuple-element.25, ...), kind=kOutput, calls=%fused_computation.40 | convolution fusion | flops 285343744 | bytes 9203712 | tf_op jit(solution)/shard_map/hqk,khd->hdq/dot_general | solution.py:60
  116.7 3.6 %fusion.39 = bf16[64,1024]{1,0:T(8,128)(2,1)} fusion(f32[64,1024]{1,0:T(8,128)S(1)} %fusion.33, f32[1024,2048]{1,0:T(8,128)S(1)} %get-tuple-element.41, f32[1024]{0:T(1024)S(1)} %get-tuple-element.37, s32[2048]{0:T(1024)S(1)} %iota_add_fusion, s32[2048]{0:T(1024)S(1)} %bitcast.105, s32[1024]{0:T(1024)S(1)} %iota_add_fusion.1, s32[1024]{0:T(1024)S(1)} %copy-done.4, ...), kind=kOutput, calls=%fused_computation.43 | convolution fusion | flops 285409280 | bytes 9338880 | tf_op jit(solution)/shard_map/hqk,khd->hdq/dot_general | solution.py:60
  120.4 17.5 %all-gather.13.cloned.1.call-done = bf16[640,2304]{1,0:T(8,128)(2,1)} async-done(((bf16[80,2304]{1,0:T(8,128)(2,1)}), bf16[640,2304]{1,0:T(8,128)(2,1)}) %all-gather.13.cloned.1.call-update) | async-done | bytes 2949136 | tf_op jit(solution)/shard_map/all_gather | solution.py:151
  137.8 1.8 slice.115
  139.8 1.1 slice.116
  140.9 6.7 %copy.49 = bf16[8,16,2304]{0,2,1:T(8,128)(2,1)} copy(bf16[8,16,2304]{2,1,0:T(8,128)(2,1)S(1)} %slice.116) | data formatting | bytes 1179648 | tf_op jit(solution)/shard_map/slice | solution.py:159
  150.3 10.6 %all-gather.9.cloned.1.call-done = bf16[512,1024]{1,0:T(8,128)(2,1)} async-done(((bf16[64,1024]{1,0:T(8,128)(2,1)}), bf16[512,1024]{1,0:T(8,128)(2,1)}) %all-gather.9.cloned.1.call-update) | async-done | bytes 1048592 | tf_op jit(solution)/shard_map/all_gather | solution.py:177
  160.9 6.1 %multiply_reduce_fusion = (f32[1024]{0:T(1024)S(1)}, f32[1024,2304]{1,0:T(8,128)S(1)}) fusion(bf16[512,1024]{1,0:T(8,128)(2,1)} %all-gather.9.cloned.1.call-done, bf16[512,2304]{1,0:T(8,128)(2,1)S(1)} %bitcast.92, bf16[1024,2304]{1,0:T(8,128)(2,1)} %all-gather.7.cloned.1.call-done), kind=kOutput, calls=%fused_computation.13 | convolution fusion | flops 2425355264 | bytes 17567744 | tf_op jit(solution)/shard_map/dot_general | solution.py:176
  168.7 1.9 copy-done.2
  170.6 1.9 fusion.92
  172.9 11.8 %fusion.2 = f32[512,2880]{0,1:T(8,128)} fusion(bf16[512,2304]{1,0:T(8,128)(2,1)S(1)} %bitcast.87, bf16[2,2880,2304]{2,1,0:T(8,128)(2,1)} %param.16), kind=kOutput, calls=%fused_computation.5 | convolution fusion | flops 6794772480 | bytes 21528576 | tf_op jit(solution)/shard_map/dot_general | solution.py:100
  184.7 22.0 %fusion.18 = bf16[512,2304]{1,0:T(8,128)(2,1)} fusion(bf16[2880,2304]{1,0:T(8,128)(2,1)} %param.17, f32[512]{0:T(512)S(1)} %mul.197, f32[512,2880]{0,1:T(8,128)} %fusion.2, bf16[512,2304]{1,0:T(8,128)(2,1)S(1)} %bitcast.88, bf16[2,2880,2304]{2,1,0:T(8,128)(2,1)} %param.16), kind=kOutput, calls=%fused_computation.30 | convolution fusion | flops 13600751616 | bytes 37160960 | tf_op jit(solution)/shard_map/dot_general | solution.py:105
  206.8 5.3 %convolution_convert_fusion = bf16[8,128,2304]{2,1,0:T(8,128)(2,1)} fusion(bf16[8,64,2304]{2,1,0:T(8,128)(2,1)} %bitcast.91, s32[8,128]{1,0:T(8,128)S(1)} %broadcast_add_fusion, pred[8,128]{1,0:T(8,128)(4,1)S(1)} %get-tuple-element.39), kind=kOutput, calls=%fused_computation.24 | convolution fusion | flops 304480256 | bytes 7083008 | tf_op jit(solution)/shard_map/sjr,sjd->srd/dot_general | solution.py:210
  212.9 53.9 %reduce-scatter.2.cloned.1.call-done = bf16[128,2304]{1,0:T(8,128)(2,1)} async-done(((bf16[1024,2304]{1,0:T(8,128)(2,1)}), bf16[128,2304]{1,0:T(8,128)(2,1)}) %reduce-scatter.2.cloned.1.call-update) | async-done | bytes 589840 | tf_op jit(solution)/shard_map/reduce_scatter | solution.py:216
  266.9 2.4 add_convert_fusion
  (72 shorter events, 11.5 us)
Async XLA Ops:
  7.2 60.3 %copy-start = (bf16[3,2304,64]{1,2,0:T(8,128)(2,1)S(1)}, bf16[3,2304,64]{1,2,0:T(8,128)(2,1)}, u32[]{:S(2)}) copy-start(bf16[3,2304,64]{1,2,0:T(8,128)(2,1)} %param.13) | copy-start | bytes 2654212
  7.2 56.9 %all-gather.7.cloned.1.call-start = ((), (), s32[]{:S(2)}) async-start(), calls=%async_computation.1 | async-start | bytes 5308416 | tf_op jit(solution)/shard_map/all_gather | solution.py:128
  7.9 91.0 %all-gather.11.cloned.1.call-start = ((), (), s32[]{:S(2)}) async-start(), calls=%async_computation.4 | async-start | bytes 1331200 | tf_op jit(solution)/shard_map/all_gather | solution.py:150
  72.3 30.0 %copy-start.4 = (s32[1024]{0:T(1024)S(1)}, s32[1024]{0:T(1024)}, u32[]{:S(2)}) copy-start(s32[1024]{0:T(1024)} %param.18) | copy-start | bytes 12292
  73.2 64.7 %all-gather.13.cloned.1.call-start = ((), (), s32[]{:S(2)}) async-start(), calls=%async_computation.5 | async-start | bytes 3317760 | tf_op jit(solution)/shard_map/all_gather | solution.py:151
  73.9 87.0 %all-gather.9.cloned.1.call-start = ((), (), s32[]{:S(2)}) async-start(), calls=%async_computation.2 | async-start | bytes 1179648 | tf_op jit(solution)/shard_map/all_gather | solution.py:177
  139.7 127.2 %reduce-scatter.2.cloned.1.call-start = ((), (), s32[]{:S(2)}) async-start(), calls=%async_computation.3 | async-start | bytes 5308416 | tf_op jit(solution)/shard_map/reduce_scatter | solution.py:216
  150.3 16.7 %copy-start.5 = (f32[2304]{0:T(1024)S(1)}, f32[2304]{0:T(1024)}, u32[]{:S(2)}) copy-start(f32[2304]{0:T(1024)} %param.12) | copy-start | bytes 27652
  167.0 3.6 %copy-start.2 = (f32[1024,2304]{1,0:T(8,128)}, f32[1024,2304]{1,0:T(8,128)S(1)}, u32[]{:S(2)}) copy-start(f32[1024,2304]{1,0:T(8,128)S(1)} %get-tuple-element.43) | copy-start | bytes 28311556
  167.0 3.6 %copy-start.3 = (f32[2304,8]{0,1:T(8,128)S(1)}, f32[2304,8]{0,1:T(8,128)}, u32[]{:S(2)}) copy-start(f32[2304,8]{0,1:T(8,128)} %param.15) | copy-start | bytes 221188
  184.7 84.5 %copy-start.1 = (bf16[3,2304,64]{1,2,0:T(8,128)(2,1)S(1)}, bf16[3,2304,64]{1,2,0:T(8,128)(2,1)}, u32[]{:S(2)}) copy-start(bf16[3,2304,64]{1,2,0:T(8,128)(2,1)} %param.13) | copy-start | bytes 2654212
Sparse Core Ops, SparseCore 0:
  9.7 54.3 all-gather.6
  73.3 25.5 all-gather.10
  101.1 36.6 all-gather.12
  139.9 20.9 all-gather.8
  212.2 54.5 reduce-scatter.1

commit v4 on v3

--- a/solution.py
+++ b/solution.py
@@ -74,7 +74,9 @@
 
 
 def unpack_ids(packed, count):
-    return packed.reshape(packed.shape[0], -1)[:, :count].astype(jnp.int32)
+    row_count = -(-count // packed.shape[-1])
+    used = packed[..., :row_count, :]
+    return used.reshape(packed.shape[:-2] + (-1,))[..., :count].astype(jnp.int32)
 
 
 def slot_table(token_ids, target, slot_count):
@@ -147,15 +149,11 @@
     kv_packed = jnp.concatenate([kv_flat, pack_ids(segment_ids, 2 * HD)], axis=0)
     out_packed = jnp.concatenate([w_out, pack_ids(expert_ids, model_width)], axis=0)
     kv_packed, out_packed = lax.optimization_barrier((kv_packed, out_packed))
-    kv_gathered = lax.all_gather(kv_packed, "seq", axis=0)
+    arrivals = []
+    for step in range(1, seq_count):
+        pairs = [(i, i ^ step) for i in range(seq_count)]
+        arrivals.append((lax.ppermute(kv_packed, "seq", pairs), seq_place ^ step))
     out_gathered = lax.all_gather(out_packed, "tensor", axis=0)
-    all_segments = unpack_ids(kv_gathered[:, kv_flat.shape[0] :], group_rows).reshape(-1)
-    all_kv = (
-        kv_gathered[:, : kv_flat.shape[0]]
-        .reshape(seq_count, head_count, group_rows, 2 * HD)
-        .transpose(0, 2, 1, 3)
-        .reshape(seq_count * group_rows, head_count, 2 * HD)
-    )
     full_ids = unpack_ids(out_gathered[:, w_out.shape[0] :], 2 * local_rows)
     w_out_full = out_gathered[:, : w_out.shape[0]].reshape(-1, model_width)
     start_state = (
@@ -164,8 +162,26 @@
         jnp.zeros((head_count, HD, group_rows), jnp.float32),
     )
     softmax_state = fold_keys(
-        start_state, query_rows, segment_ids, positions, all_kv, all_segments, jnp.int32(0)
-    )
+        start_state,
+        query_rows,
+        segment_ids,
+        positions,
+        kv_rows,
+        segment_ids,
+        seq_place * group_rows,
+    )
+    for arrived, source in arrivals:
+        softmax_state = fold_keys(
+            softmax_state,
+            query_rows,
+            segment_ids,
+            positions,
+            arrived[: kv_flat.shape[0]]
+            .reshape(head_count, group_rows, 2 * HD)
+            .transpose(1, 0, 2),
+            unpack_ids(arrived[kv_flat.shape[0] :], group_rows),
+            source * group_rows,
+        )
     running_max, denominator, weighted_sum = softmax_state
     attended = (
         (weighted_sum / denominator[:, None, :])

time: 276 us -> 257 us (0.931); the launches traced: 276 us -> 253 us
  waiting for transfers between devices: 161 us -> 141 us
  local copies, waits for them, and re-layouts: 16.4 us -> 8.3 us
  starting transfers between devices: 0.2 us -> 4.45 us
  matrix products: 65.1 us -> 67.9 us
    all_gather x1 -> x0, waiting for transfers between devices: 25 us -> none  [shards(): kv_gathered = lax.all_gather(kv_packed, 'seq', axis=0)]
    all_gather x1, waiting for transfers between devices: 17.5 us -> 5.55 us  [shards(): out_gathered = lax.all_gather(out_packed, 'tensor', axis=0)]
    ppermute x0 -> x3, waiting for transfers between devices: none -> 8.72 us  [shards(): arrivals.append((lax.ppermute(kv_packed, 'seq', pairs), seq_place ^ step))]
    slice x3 -> x2, local copies, waits for them, and re-layouts: 9.04 us -> 1.04 us  [the longest x1 1 us: unpack_ids(): used = packed[..., :row_count, :]]
    all_gather x1, waiting for transfers between devices: 10.6 us -> 18.5 us  [shards(): lax.all_gather(attended, 'tensor', axis=0, tiled=True)]
    reduce_sum x1, other arithmetic: 6.46 us -> 1.77 us  [fold_keys(): denominator = denominator * factor + jnp.sum(weights, axis=-1)]
    dot_general x2 -> x4, matrix products: 6.03 us -> 10.5 us  [fold_keys(): jnp.einsum('qhd,khd->hqk', query_rows, key_block, preferred_element_type=...]
    ppermute x0 -> x3, starting transfers between devices: none -> 3.55 us  [shards(): arrivals.append((lax.ppermute(kv_packed, 'seq', pairs), seq_place ^ step))]
  transfers between devices with their start and end apart: 5 -> 7, of which waited for: 5 -> 6; matrix products, arithmetic and copies ran while one was open for 13% -> 10% of each run, Pallas kernels for 0% -> 0%
where the time goes in v4:
time: 257 us; the launch traced here: 253 us
  waiting for transfers between devices  141 us (55%)
  matrix products  67.9 us (26%)
  other arithmetic  17.5 us (7%)
  between operations  14.4 us (6%)
  local copies, waits for them, and re-layouts  8.3 us (3%)
  starting transfers between devices  4.45 us (2%)
    reduce_scatter x1, waiting for transfers between devices, shards(): lax.psum_scatter(placed.astype(jnp.bfloat16), 'tensor', scatter_dimension...  54.7 us
    all_gather x1, waiting for transfers between devices, shards(): full_hidden = lax.all_gather(hidden_in, 'tensor', axis=0, tiled=True)  52.5 us
    dot_general x1, matrix products, expert_apply(): output = jnp.dot(hidden_act, w_down, preferred_element_type=jnp.float32)  22 us
    all_gather x1, waiting for transfers between devices, shards(): lax.all_gather(attended, 'tensor', axis=0, tiled=True)  18.5 us
    dot_general x1, matrix products, expert_apply(): lax.dot_general(slot_rows, w_gate_up[0], contract, preferred_element_type...  12 us
    dot_general x4, matrix products, fold_keys(): jnp.einsum('qhd,khd->hqk', query_rows, key_block, preferred_element_type=...  10.5 us
    ppermute x3, waiting for transfers between devices, shards(): arrivals.append((lax.ppermute(kv_packed, 'seq', pairs), seq_place ^ step))  8.72 us
    dot_general x4, matrix products, fold_keys(): jnp.einsum('hqk,khd->hdq', weights.astype(jnp.bfloat16), value_block, pre...  7.19 us
  transfers between devices with their start and end apart: 7, of which 6 were waited for; matrix products, arithmetic and copies ran while one was open for 10% of the time, Pallas kernels for 0%

profile of v4, /device:TPU:0, one launch (start us, length us, event | category | flops | bytes accessed | tf_op | source)
XLA Modules:
  0.0 253.3 jit_solution(6927243527488938776)
XLA Ops:
  9.9 1.7 pad_maximum_fusion
  11.6 52.5 %all-gather.5.cloned.1.call-done = bf16[1024,2304]{1,0:T(8,128)(2,1)} async-done(((bf16[128,2304]{1,0:T(8,128)(2,1)}), bf16[1024,2304]{1,0:T(8,128)(2,1)}) %all-gather.5.cloned.1.call-update) | async-done | bytes 4718608 | tf_op jit(solution)/shard_map/all_gather | solution.py:130
  64.1 3.5 %fusion.6 = f32[1024]{0:T(1024)S(1)} fusion(bf16[1024,2304]{1,0:T(8,128)(2,1)} %all-gather.5.cloned.1.call-done), kind=kLoop, calls=%fused_computation.9 | loop fusion | flops 7076864 | bytes 4722688 | tf_op jit(solution)/shard_map/reduce_sum | solution.py:17
  67.9 1.8 fusion.11
  70.8 3.1 %fusion.76 = (bf16[1024,1,32]{2,0,1:T(8,128)(2,1)S(1)}, bf16[1024,1,32]{2,0,1:T(8,128)(2,1)S(1)}, bf16[1024,32]{1,0:T(8,128)(2,1)S(1)}, bf16[1024,32]{1,0:T(8,128)(2,1)}) fusion(f32[1024,1,32]{2,0,1:T(8,128)S(1)} %copy.84, f32[1024,1,32]{2,0,1:T(8,128)S(1)} %copy.83, f32[32]{0:T(128)S(1)} %multiply_exponential_fusion, f32[1024]{0:T(1024)S(1)} %fusion.107, ...), kind=kLoop, calls=%fused_computation.76 | loop fusion | flops 557056 | bytes 790656 | tf_op jit(solution)/shard_map/convert.9
  80.9 3.3 %collective-permute-done = bf16[1040,128]{1,0:T(8,128)(2,1)S(1)} collective-permute-done((bf16[1040,128]{1,0:T(8,128)(2,1)S(1)}, bf16[1040,128]{1,0:T(8,128)(2,1)S(1)}, u32[]{:S(2)}, u32[]{:S(2)}) %collective-permute-start) | collective-permute-done | bytes 266272 | tf_op jit(solution)/shard_map/ppermute | solution.py:155
  84.9 5.5 %collective-permute-done.1 = bf16[1040,128]{1,0:T(8,128)(2,1)S(1)} collective-permute-done((bf16[1040,128]{1,0:T(8,128)(2,1)S(1)}, bf16[1040,128]{1,0:T(8,128)(2,1)S(1)}, u32[]{:S(2)}, u32[]{:S(2)}) %collective-permute-start.1) | collective-permute-done | bytes 266272 | tf_op jit(solution)/shard_map/ppermute | solution.py:155
  90.4 3.2 %fusion.18 = (f32[1024]{0:T(1024)S(1)}, f32[1024]{0:T(1024)S(1)}, f32[1024]{0:T(1024)S(1)}, f32[1024,1024]{0,1:T(8,128)S(1)}) fusion(s32[1024]{0:T(1024)S(1)} %get-tuple-element.56, s32[1024]{0:T(1024)S(1)} %copy-done.5, s32[1024]{0:T(1024)S(1)} %get-tuple-element.58, s32[1024]{0:T(1024)S(1)} %fusion.105, f32[1024,1024]{0,1:T(8,128)S(1)} %fusion.84, ...), kind=kOutput, calls=%fused_computation.36 | convolution fusion | flops 153089024 | bytes 13152256 | tf_op jit(solution)/shard_map/qhd,khd->hqk/dot_general | solution.py:49
  93.6 5.9 %fusion.20 = (f32[1024]{0:T(1024)S(1)}, f32[1024]{0:T(1024)S(1)}, f32[1024]{0:T(1024)S(1)}, f32[1024]{0:T(1024)S(1)}, f32[1024,1024]{0,1:T(8,128)S(1)}) fusion(f32[1024,1024]{0,1:T(8,128)S(1)} %fusion.84, f32[1024]{0:T(1024)S(1)} %get-tuple-element.46, s32[1024]{0:T(1024)S(1)} %get-tuple-element.56, s32[1024]{0:T(1024)S(1)} %copy-done.5, ...), kind=kOutput, calls=%fused_computation.38 | convolution fusion | flops 165670912 | bytes 17371136 | tf_op jit(solution)/shard_map/qhd,khd->hqk/dot_general | solution.py:49
  99.5 1.8 fusion.26
  101.3 1.8 fusion.32
  103.1 1.8 fusion.30
  106.3 2.2 fusion.60
  108.5 5.5 %all-gather.9.cloned.1.call-done = bf16[640,2304]{1,0:T(8,128)(2,1)} async-done(((bf16[80,2304]{1,0:T(8,128)(2,1)}), bf16[640,2304]{1,0:T(8,128)(2,1)}) %all-gather.9.cloned.1.call-update) | async-done | bytes 2949136 | tf_op jit(solution)/shard_map/all_gather | solution.py:156
  114.1 1.8 slice.120
  118.5 18.5 %all-gather.7.cloned.1.call-done = bf16[512,1024]{1,0:T(8,128)(2,1)} async-done(((bf16[64,1024]{1,0:T(8,128)(2,1)}), bf16[512,1024]{1,0:T(8,128)(2,1)}) %all-gather.7.cloned.1.call-update) | async-done | bytes 1048592 | tf_op jit(solution)/shard_map/all_gather | solution.py:193
  137.1 6.1 %multiply_reduce_fusion = (f32[1024]{0:T(1024)S(1)}, f32[1024,2304]{1,0:T(8,128)S(1)}) fusion(bf16[512,1024]{1,0:T(8,128)(2,1)} %all-gather.7.cloned.1.call-done, bf16[512,2304]{1,0:T(8,128)(2,1)S(1)} %bitcast.110, bf16[1024,2304]{1,0:T(8,128)(2,1)} %all-gather.5.cloned.1.call-done), kind=kOutput, calls=%fused_computation.13 | convolution fusion | flops 2425355264 | bytes 17567744 | tf_op jit(solution)/shard_map/dot_general | solution.py:192
  144.1 2.7 %copy-done.2 = f32[1024,2304]{1,0:T(8,128)} copy-done((f32[1024,2304]{1,0:T(8,128)}, f32[1024,2304]{1,0:T(8,128)S(1)}, u32[]{:S(2)}) %copy-start.2) | copy-done | bytes 9437208
  147.7 1.9 fusion.129
  149.8 12.0 %fusion.2 = f32[512,2880]{0,1:T(8,128)} fusion(bf16[512,2304]{1,0:T(8,128)(2,1)S(1)} %bitcast.107, bf16[2,2880,2304]{2,1,0:T(8,128)(2,1)} %param.16), kind=kOutput, calls=%fused_computation.5 | convolution fusion | flops 6794772480 | bytes 21528576 | tf_op jit(solution)/shard_map/dot_general | solution.py:102
  162.0 22.0 %fusion.15 = bf16[512,2304]{1,0:T(8,128)(2,1)} fusion(bf16[2880,2304]{1,0:T(8,128)(2,1)} %param.17, f32[512]{0:T(512)S(1)} %mul.262, f32[512,2880]{0,1:T(8,128)} %fusion.2, bf16[512,2304]{1,0:T(8,128)(2,1)S(1)} %bitcast.108, bf16[2,2880,2304]{2,1,0:T(8,128)(2,1)} %param.16), kind=kOutput, calls=%fused_computation.21 | convolution fusion | flops 13600751616 | bytes 37160960 | tf_op jit(solution)/shard_map/dot_general | solution.py:107
  184.0 5.4 %convolution_convert_fusion = bf16[8,128,2304]{2,1,0:T(8,128)(2,1)} fusion(bf16[8,64,2304]{2,1,0:T(8,128)(2,1)} %bitcast.109, s32[8,128]{1,0:T(8,128)S(1)} %broadcast_add_fusion, pred[8,128]{1,0:T(8,128)(4,1)S(1)} %get-tuple-element.47), kind=kOutput, calls=%fused_computation.15 | convolution fusion | flops 304480256 | bytes 7083008 | tf_op jit(solution)/shard_map/sjr,sjd->srd/dot_general | solution.py:226
  189.4 54.7 %reduce-scatter.2.cloned.1.call-done = bf16[128,2304]{1,0:T(8,128)(2,1)} async-done(((bf16[1024,2304]{1,0:T(8,128)(2,1)}), bf16[128,2304]{1,0:T(8,128)(2,1)}) %reduce-scatter.2.cloned.1.call-update) | async-done | bytes 589840 | tf_op jit(solution)/shard_map/reduce_scatter | solution.py:232
  244.2 2.4 add_convert_fusion
  (89 shorter events, 17.8 us)
Async XLA Ops:
  7.2 60.4 %copy-start = (bf16[3,2304,64]{1,2,0:T(8,128)(2,1)S(1)}, bf16[3,2304,64]{1,2,0:T(8,128)(2,1)}, u32[]{:S(2)}) copy-start(bf16[3,2304,64]{1,2,0:T(8,128)(2,1)} %param.13) | copy-start | bytes 2654212
  7.2 60.4 %copy-start.7 = (f32[2304]{0:T(1024)S(1)}, f32[2304]{0:T(1024)}, u32[]{:S(2)}) copy-start(f32[2304]{0:T(1024)} %param.11) | copy-start | bytes 27652
  7.2 56.9 %all-gather.5.cloned.1.call-start = ((), (), s32[]{:S(2)}) async-start(), calls=%async_computation.1 | async-start | bytes 5308416 | tf_op jit(solution)/shard_map/all_gather | solution.py:130
  7.9 106.1 %all-gather.9.cloned.1.call-start = ((), (), s32[]{:S(2)}) async-start(), calls=%async_computation.4 | async-start | bytes 3317760 | tf_op jit(solution)/shard_map/all_gather | solution.py:156
  64.1 3.8 %copy-start.3 = (bf16[1024,2304]{1,0:T(8,128)(2,1)S(1)}, bf16[1024,2304]{1,0:T(8,128)(2,1)}, u32[]{:S(2)}) copy-start(bf16[1024,2304]{1,0:T(8,128)(2,1)} %all-gather.5.cloned.1.call-done) | copy-start | bytes 14155780
  74.8 9.3 %collective-permute-start = (bf16[1040,128]{1,0:T(8,128)(2,1)S(1)}, bf16[1040,128]{1,0:T(8,128)(2,1)S(1)}, u32[]{:S(2)}, u32[]{:S(2)}) collective-permute-start(bf16[1040,128]{1,0:T(8,128)(2,1)S(1)} %pad_maximum_fusion.1), channel_id=1, source_target_pairs={{0,8},{8,0},{16,24},{24,16},{1,9},{9,1},{17,25},{25,17},{2,10},{10... | collective-permute-start | bytes 798728 | tf_op jit(solution)/shard_map/ppermute | solution.py:155
  76.4 14.0 %collective-permute-start.1 = (bf16[1040,128]{1,0:T(8,128)(2,1)S(1)}, bf16[1040,128]{1,0:T(8,128)(2,1)S(1)}, u32[]{:S(2)}, u32[]{:S(2)}) collective-permute-start(bf16[1040,128]{1,0:T(8,128)(2,1)S(1)} %pad_maximum_fusion.1), channel_id=1, source_target_pairs={{0,16},{8,24},{16,0},{24,8},{1,17},{9,25},{17,1},{25,9},{2,18},{10... | collective-permute-start | bytes 798728 | tf_op jit(solution)/shard_map/ppermute | solution.py:155
  77.9 15.7 %collective-permute-start.2 = (bf16[1040,128]{1,0:T(8,128)(2,1)S(1)}, bf16[1040,128]{1,0:T(8,128)(2,1)S(1)}, u32[]{:S(2)}, u32[]{:S(2)}) collective-permute-start(bf16[1040,128]{1,0:T(8,128)(2,1)S(1)} %pad_maximum_fusion.1), channel_id=1, source_target_pairs={{0,24},{8,16},{16,8},{24,0},{1,25},{9,17},{17,9},{25,1},{2,26},{10... | collective-permute-start | bytes 798728 | tf_op jit(solution)/shard_map/ppermute | solution.py:155
  78.4 58.6 %all-gather.7.cloned.1.call-start = ((), (), s32[]{:S(2)}) async-start(), calls=%async_computation.2 | async-start | bytes 1179648 | tf_op jit(solution)/shard_map/all_gather | solution.py:193
  80.1 10.3 %copy-start.5 = (s32[1024]{0:T(1024)S(1)}, s32[1024]{0:T(1024)}, u32[]{:S(2)}) copy-start(s32[1024]{0:T(1024)} %param.18) | copy-start | bytes 12292
  115.9 128.2 %reduce-scatter.2.cloned.1.call-start = ((), (), s32[]{:S(2)}) async-start(), calls=%async_computation.3 | async-start | bytes 5308416 | tf_op jit(solution)/shard_map/reduce_scatter | solution.py:232
  118.5 24.6 %copy-start.6 = (f32[2304]{0:T(1024)S(1)}, f32[2304]{0:T(1024)}, u32[]{:S(2)}) copy-start(f32[2304]{0:T(1024)} %param.12) | copy-start | bytes 27652
  143.1 3.6 %copy-start.2 = (f32[1024,2304]{1,0:T(8,128)}, f32[1024,2304]{1,0:T(8,128)S(1)}, u32[]{:S(2)}) copy-start(f32[1024,2304]{1,0:T(8,128)S(1)} %get-tuple-element.52) | copy-start | bytes 28311556
  146.8 0.9 copy-start.4
  184.0 62.5 %copy-start.1 = (bf16[3,2304,64]{1,2,0:T(8,128)(2,1)S(1)}, bf16[3,2304,64]{1,2,0:T(8,128)(2,1)}, u32[]{:S(2)}) copy-start(bf16[3,2304,64]{1,2,0:T(8,128)(2,1)} %param.13) | copy-start | bytes 2654212
Sparse Core Ops, SparseCore 0:
  9.7 54.3 all-gather.4
  78.5 35.4 all-gather.8
  116.1 20.9 all-gather.6
  189.5 54.5 reduce-scatter.1

commit v5 on v4

--- a/solution.py
+++ b/solution.py
@@ -1,8 +1,11 @@
+import functools
 import math
 
 import jax
 import jax.numpy as jnp
 from jax import lax
+from jax.experimental import pallas as pl
+from jax.experimental.pallas import tpu as pltpu
 from jax.sharding import PartitionSpec as P
 
 HD = 64
@@ -89,6 +92,51 @@
     return chosen_slot.astype(jnp.bfloat16)
 
 
+def ffn_kernel(step_count, rows_ref, weight_ref, gate_up_ref, down_ref, out_ref, total_ref):
+    step = pl.program_id(0)
+    contract = (((1,), (1,)), ((), ()))
+    rows = rows_ref[...]
+    gate_act = lax.dot_general(rows, gate_up_ref[0], contract, preferred_element_type=jnp.float32)
+    up_act = lax.dot_general(rows, gate_up_ref[1], contract, preferred_element_type=jnp.float32)
+    hidden_act = (gate_act / (1.0 + jnp.exp(-gate_act)) * up_act).astype(jnp.bfloat16)
+
+    @pl.when(step == 0)
+    def _():
+        total_ref[...] = jnp.zeros_like(total_ref)
+
+    total_ref[...] += jnp.dot(hidden_act, down_ref[...], preferred_element_type=jnp.float32)
+
+    @pl.when(step == step_count - 1)
+    def _():
+        out_ref[...] = (total_ref[...] * weight_ref[...]).astype(out_ref.dtype)
+
+
+def feed_forward(rows, weight, w_gate_up, w_down):
+    row_count, model_width = rows.shape
+    hidden_count = w_down.shape[0]
+    tile = max(t for t in range(16, 513, 16) if hidden_count % t == 0)
+    step_count = hidden_count // tile
+    return pl.pallas_call(
+        functools.partial(ffn_kernel, step_count),
+        grid=(step_count,),
+        in_specs=[
+            pl.BlockSpec((row_count, model_width), lambda j: (0, 0)),
+            pl.BlockSpec((row_count, 1), lambda j: (0, 0)),
+            pl.BlockSpec((2, tile, model_width), lambda j: (0, j, 0)),
+            pl.BlockSpec((tile, model_width), lambda j: (j, 0)),
+        ],
+        out_specs=pl.BlockSpec((row_count, model_width), lambda j: (0, 0)),
+        out_shape=jax.ShapeDtypeStruct((row_count, model_width), jnp.bfloat16),
+        scratch_shapes=[pltpu.VMEM((row_count, model_width), jnp.float32)],
+        compiler_params=pltpu.CompilerParams(vmem_limit_bytes=48 * 1024 * 1024),
+        cost_estimate=pl.CostEstimate(
+            flops=6 * row_count * model_width * hidden_count,
+            bytes_accessed=6 * model_width * hidden_count,
+            transcendentals=row_count * hidden_count,
+        ),
+    )(rows, weight, w_gate_up, w_down)
+
+
 def expert_apply(slot_rows, slot_ids, own_expert, w_router, w_gate_up, w_down):
     logits = jnp.dot(slot_rows.astype(jnp.float32), w_router, precision=lax.Precision.HIGHEST)
     expert_count = w_router.shape[1]
@@ -98,14 +146,7 @@
     chosen = jnp.sum(one_hot * logits[:, None, :], axis=-1)
     gate_probs = jax.nn.softmax(chosen, axis=-1)
     weight = jnp.sum(jnp.where(slot_ids == own_expert, gate_probs, 0.0), axis=-1)
-    contract = (((1,), (1,)), ((), ()))
-    gate_act = lax.dot_general(
-        slot_rows, w_gate_up[0], contract, preferred_element_type=jnp.float32
-    )
-    up_act = lax.dot_general(slot_rows, w_gate_up[1], contract, preferred_element_type=jnp.float32)
-    hidden_act = (jax.nn.silu(gate_act) * up_act).astype(jnp.bfloat16)
-    output = jnp.dot(hidden_act, w_down, preferred_element_type=jnp.float32)
-    return (output * weight[:, None]).astype(jnp.bfloat16)
+    return feed_forward(slot_rows, weight[:, None], w_gate_up, w_down)
 
 
 def shards(

time: 257 us -> 246 us (0.957); the launches traced: 253 us -> 246 us
  matrix products: 67.9 us -> 32.2 us
  Pallas kernels: 0 us -> 28.1 us
    dot_general x2 -> x0, matrix products: 34 us -> none  [the longest x1 22 us: expert_apply(): output = jnp.dot(hidden_act, w_down, preferred_element_type=jnp.float32)]
    pallas_call x0 -> x1, Pallas kernels: none -> 28.1 us  [feed_forward(): pl.pallas_call(functools.partial(ffn_kernel, step_count), grid=(step_coun...]
  transfers between devices with their start and end apart: 7 -> 7, of which waited for: 6 -> 6; matrix products, arithmetic and copies ran while one was open for 10% -> 11% of each run, Pallas kernels for 0% -> 0%
where the time goes in v5:
time: 246 us
  waiting for transfers between devices  141 us (57%)
  matrix products  32.2 us (13%)
  Pallas kernels  28.1 us (11%)
  other arithmetic  17.5 us (7%)
  between operations  14.2 us (6%)
  local copies, waits for them, and re-layouts  8.44 us (3%)
  starting transfers between devices  4.15 us (2%)
    reduce_scatter x1, waiting for transfers between devices, shards(): lax.psum_scatter(placed.astype(jnp.bfloat16), 'tensor', scatter_dimension...  54.7 us
    all_gather x1, waiting for transfers between devices, shards(): full_hidden = lax.all_gather(hidden_in, 'tensor', axis=0, tiled=True)  52.5 us
    pallas_call x1, Pallas kernels, feed_forward(): pl.pallas_call(functools.partial(ffn_kernel, step_count), grid=(step_coun...  28.1 us
    all_gather x1, waiting for transfers between devices, shards(): lax.all_gather(attended, 'tensor', axis=0, tiled=True)  18.5 us
    dot_general x4, matrix products, fold_keys(): jnp.einsum('qhd,khd->hqk', query_rows, key_block, preferred_element_type=...  10.5 us
    ppermute x3, waiting for transfers between devices, shards(): arrivals.append((lax.ppermute(kv_packed, 'seq', pairs), seq_place ^ step))  9.07 us
    dot_general x4, matrix products, fold_keys(): jnp.einsum('hqk,khd->hdq', weights.astype(jnp.bfloat16), value_block, pre...  7.19 us
    dot_general x1, matrix products, shards(): lax.dot_general(lax.all_gather(attended, 'tensor', axis=0, tiled=True), w...  6.09 us
  transfers between devices with their start and end apart: 7, of which 6 were waited for; matrix products, arithmetic and copies ran while one was open for 11% of the time, Pallas kernels for 0%

profile of v5, /device:TPU:0, one launch (start us, length us, event | category | flops | bytes accessed | tf_op | source)
XLA Modules:
  0.0 245.7 jit_solution(7924727834647974621)
XLA Ops:
  9.9 1.7 pad_maximum_fusion
  11.6 52.5 %all-gather.5.cloned.1.call-done = bf16[1024,2304]{1,0:T(8,128)(2,1)} async-done(((bf16[128,2304]{1,0:T(8,128)(2,1)}), bf16[1024,2304]{1,0:T(8,128)(2,1)}) %all-gather.5.cloned.1.call-update) | async-done | bytes 4718608 | tf_op jit(solution)/shard_map/all_gather | solution.py:171
  64.1 3.5 %fusion = f32[1024]{0:T(1024)S(1)} fusion(bf16[1024,2304]{1,0:T(8,128)(2,1)} %all-gather.5.cloned.1.call-done), kind=kLoop, calls=%fused_computation.3 | loop fusion | flops 7076864 | bytes 4722688 | tf_op jit(solution)/shard_map/reduce_sum | solution.py:20
  67.9 1.8 fusion.3
  70.8 3.1 %fusion.67 = (bf16[1024,1,32]{2,0,1:T(8,128)(2,1)S(1)}, bf16[1024,1,32]{2,0,1:T(8,128)(2,1)S(1)}, bf16[1024,32]{1,0:T(8,128)(2,1)S(1)}, bf16[1024,32]{1,0:T(8,128)(2,1)}) fusion(f32[1024,1,32]{2,0,1:T(8,128)S(1)} %copy.89, f32[1024,1,32]{2,0,1:T(8,128)S(1)} %copy.88, f32[32]{0:T(128)S(1)} %multiply_exponential_fusion, f32[1024]{0:T(1024)S(1)} %fusion.98, ...), kind=kLoop, calls=%fused_computation.67 | loop fusion | flops 557056 | bytes 790656 | tf_op jit(solution)/shard_map/convert.9
  74.9 1.5 collective-permute-start
  80.5 3.6 %collective-permute-done = bf16[1040,128]{1,0:T(8,128)(2,1)S(1)} collective-permute-done((bf16[1040,128]{1,0:T(8,128)(2,1)S(1)}, bf16[1040,128]{1,0:T(8,128)(2,1)S(1)}, u32[]{:S(2)}, u32[]{:S(2)}) %collective-permute-start) | collective-permute-done | bytes 266272 | tf_op jit(solution)/shard_map/ppermute | solution.py:196
  84.9 5.5 %collective-permute-done.1 = bf16[1040,128]{1,0:T(8,128)(2,1)S(1)} collective-permute-done((bf16[1040,128]{1,0:T(8,128)(2,1)S(1)}, bf16[1040,128]{1,0:T(8,128)(2,1)S(1)}, u32[]{:S(2)}, u32[]{:S(2)}) %collective-permute-start.1) | collective-permute-done | bytes 266272 | tf_op jit(solution)/shard_map/ppermute | solution.py:196
  90.4 3.2 %fusion.9 = (f32[1024]{0:T(1024)S(1)}, f32[1024]{0:T(1024)S(1)}, f32[1024]{0:T(1024)S(1)}, f32[1024,1024]{0,1:T(8,128)S(1)}) fusion(s32[1024]{0:T(1024)S(1)} %get-tuple-element.56, s32[1024]{0:T(1024)S(1)} %copy-done.5, s32[1024]{0:T(1024)S(1)} %get-tuple-element.58, s32[1024]{0:T(1024)S(1)} %fusion.96, f32[1024,1024]{0,1:T(8,128)S(1)} %fusion.75, ...), kind=kOutput, calls=%fused_computation.27 | convolution fusion | flops 153089024 | bytes 13152256 | tf_op jit(solution)/shard_map/qhd,khd->hqk/dot_general | solution.py:52
  93.6 5.9 %fusion.11 = (f32[1024]{0:T(1024)S(1)}, f32[1024]{0:T(1024)S(1)}, f32[1024]{0:T(1024)S(1)}, f32[1024]{0:T(1024)S(1)}, f32[1024,1024]{0,1:T(8,128)S(1)}) fusion(f32[1024,1024]{0,1:T(8,128)S(1)} %fusion.75, f32[1024]{0:T(1024)S(1)} %get-tuple-element.46, s32[1024]{0:T(1024)S(1)} %get-tuple-element.56, s32[1024]{0:T(1024)S(1)} %copy-done.5, ...), kind=kOutput, calls=%fused_computation.29 | convolution fusion | flops 165670912 | bytes 17371136 | tf_op jit(solution)/shard_map/qhd,khd->hqk/dot_general | solution.py:52
  99.5 1.8 fusion.17
  101.4 1.8 fusion.23
  103.2 1.8 fusion.21
  106.3 2.2 fusion.51
  108.6 5.5 %all-gather.9.cloned.1.call-done = bf16[640,2304]{1,0:T(8,128)(2,1)} async-done(((bf16[80,2304]{1,0:T(8,128)(2,1)}), bf16[640,2304]{1,0:T(8,128)(2,1)}) %all-gather.9.cloned.1.call-update) | async-done | bytes 2949136 | tf_op jit(solution)/shard_map/all_gather | solution.py:197
  114.1 1.8 slice.112
  118.6 18.5 %all-gather.7.cloned.1.call-done = bf16[512,1024]{1,0:T(8,128)(2,1)} async-done(((bf16[64,1024]{1,0:T(8,128)(2,1)}), bf16[512,1024]{1,0:T(8,128)(2,1)}) %all-gather.7.cloned.1.call-update) | async-done | bytes 1048592 | tf_op jit(solution)/shard_map/all_gather | solution.py:234
  137.1 6.1 %multiply_reduce_fusion = (f32[1024]{0:T(1024)S(1)}, f32[1024,2304]{1,0:T(8,128)S(1)}) fusion(bf16[512,1024]{1,0:T(8,128)(2,1)} %all-gather.7.cloned.1.call-done, bf16[512,2304]{1,0:T(8,128)(2,1)S(1)} %bitcast.96, bf16[1024,2304]{1,0:T(8,128)(2,1)} %all-gather.5.cloned.1.call-done), kind=kOutput, calls=%fused_computation.7 | convolution fusion | flops 2425355264 | bytes 17567744 | tf_op jit(solution)/shard_map/dot_general | solution.py:233
  144.1 2.7 %copy-done.2 = f32[1024,2304]{1,0:T(8,128)} copy-done((f32[1024,2304]{1,0:T(8,128)}, f32[1024,2304]{1,0:T(8,128)S(1)}, u32[]{:S(2)}) %copy-start.2) | copy-done | bytes 9437208
  147.7 1.9 fusion.118
  150.2 28.1 %shard_map.113 = bf16[512,2304]{1,0:T(8,128)(2,1)S(1)} custom-call(bf16[512,2304]{1,0:T(8,128)(2,1)S(1)} %bitcast.92, f32[512,1]{1,0:T(8,128)S(1)} %broadcast_in_dim.42.weight_ref, bf16[2,2880,2304]{2,1,0:T(8,128)(2,1)} %gate_up_ref.1, bf16[2880,2304]{1,0:T(8,128)(2,1)} %down_ref.1), custom_call_target="tpu_custom_call" | custom-call | flops 20384317440 | bytes 39813120 | tf_op jit(solution)/shard_map/pallas_call | solution.py:119
  178.3 3.7 %convolution_convert_fusion = bf16[8,128,2304]{2,1,0:T(8,128)(2,1)} fusion(bf16[8,64,2304]{2,1,0:T(8,128)(2,1)S(1)} %bitcast.93, s32[8,128]{1,0:T(8,128)S(1)} %broadcast_add_fusion, pred[8,128]{1,0:T(8,128)(4,1)S(1)} %get-tuple-element.47), kind=kOutput, calls=%fused_computation.8 | convolution fusion | flops 304480256 | bytes 7083008 | tf_op jit(solution)/shard_map/sjr,sjd->srd/dot_general | solution.py:267
  182.0 54.7 %reduce-scatter.2.cloned.1.call-done = bf16[128,2304]{1,0:T(8,128)(2,1)} async-done(((bf16[1024,2304]{1,0:T(8,128)(2,1)}), bf16[128,2304]{1,0:T(8,128)(2,1)}) %reduce-scatter.2.cloned.1.call-update) | async-done | bytes 589840 | tf_op jit(solution)/shard_map/reduce_scatter | solution.py:273
  236.8 2.4 add_convert_fusion
  (88 shorter events, 16.1 us)
Async XLA Ops:
  7.2 60.4 %copy-start = (bf16[3,2304,64]{1,2,0:T(8,128)(2,1)S(1)}, bf16[3,2304,64]{1,2,0:T(8,128)(2,1)}, u32[]{:S(2)}) copy-start(bf16[3,2304,64]{1,2,0:T(8,128)(2,1)} %param.13) | copy-start | bytes 2654212
  7.2 60.4 %copy-start.7 = (f32[2304]{0:T(1024)S(1)}, f32[2304]{0:T(1024)}, u32[]{:S(2)}) copy-start(f32[2304]{0:T(1024)} %param.11) | copy-start | bytes 27652
  7.2 56.9 %all-gather.5.cloned.1.call-start = ((), (), s32[]{:S(2)}) async-start(), calls=%async_computation.1 | async-start | bytes 5308416 | tf_op jit(solution)/shard_map/all_gather | solution.py:171
  7.9 106.2 %all-gather.9.cloned.1.call-start = ((), (), s32[]{:S(2)}) async-start(), calls=%async_computation.4 | async-start | bytes 3317760 | tf_op jit(solution)/shard_map/all_gather | solution.py:197
  64.1 3.8 %copy-start.3 = (bf16[1024,2304]{1,0:T(8,128)(2,1)S(1)}, bf16[1024,2304]{1,0:T(8,128)(2,1)}, u32[]{:S(2)}) copy-start(bf16[1024,2304]{1,0:T(8,128)(2,1)} %all-gather.5.cloned.1.call-done) | copy-start | bytes 14155780
  74.9 9.3 %collective-permute-start = (bf16[1040,128]{1,0:T(8,128)(2,1)S(1)}, bf16[1040,128]{1,0:T(8,128)(2,1)S(1)}, u32[]{:S(2)}, u32[]{:S(2)}) collective-permute-start(bf16[1040,128]{1,0:T(8,128)(2,1)S(1)} %pad_maximum_fusion.1), channel_id=1, source_target_pairs={{0,8},{8,0},{16,24},{24,16},{1,9},{9,1},{17,25},{25,17},{2,10},{10... | collective-permute-start | bytes 798728 | tf_op jit(solution)/shard_map/ppermute | solution.py:196
  76.4 14.0 %collective-permute-start.1 = (bf16[1040,128]{1,0:T(8,128)(2,1)S(1)}, bf16[1040,128]{1,0:T(8,128)(2,1)S(1)}, u32[]{:S(2)}, u32[]{:S(2)}) collective-permute-start(bf16[1040,128]{1,0:T(8,128)(2,1)S(1)} %pad_maximum_fusion.1), channel_id=1, source_target_pairs={{0,16},{8,24},{16,0},{24,8},{1,17},{9,25},{17,1},{25,9},{2,18},{10... | collective-permute-start | bytes 798728 | tf_op jit(solution)/shard_map/ppermute | solution.py:196
  77.9 15.7 %collective-permute-start.2 = (bf16[1040,128]{1,0:T(8,128)(2,1)S(1)}, bf16[1040,128]{1,0:T(8,128)(2,1)S(1)}, u32[]{:S(2)}, u32[]{:S(2)}) collective-permute-start(bf16[1040,128]{1,0:T(8,128)(2,1)S(1)} %pad_maximum_fusion.1), channel_id=1, source_target_pairs={{0,24},{8,16},{16,8},{24,0},{1,25},{9,17},{17,9},{25,1},{2,26},{10... | collective-permute-start | bytes 798728 | tf_op jit(solution)/shard_map/ppermute | solution.py:196
  78.4 58.7 %all-gather.7.cloned.1.call-start = ((), (), s32[]{:S(2)}) async-start(), calls=%async_computation.2 | async-start | bytes 1179648 | tf_op jit(solution)/shard_map/all_gather | solution.py:234
  79.8 10.6 %copy-start.5 = (s32[1024]{0:T(1024)S(1)}, s32[1024]{0:T(1024)}, u32[]{:S(2)}) copy-start(s32[1024]{0:T(1024)} %param.18) | copy-start | bytes 12292
  115.9 120.8 %reduce-scatter.2.cloned.1.call-start = ((), (), s32[]{:S(2)}) async-start(), calls=%async_computation.3 | async-start | bytes 5308416 | tf_op jit(solution)/shard_map/reduce_scatter | solution.py:273
  118.6 24.6 %copy-start.6 = (f32[2304]{0:T(1024)S(1)}, f32[2304]{0:T(1024)}, u32[]{:S(2)}) copy-start(f32[2304]{0:T(1024)} %param.12) | copy-start | bytes 27652
  143.2 3.6 %copy-start.2 = (f32[1024,2304]{1,0:T(8,128)}, f32[1024,2304]{1,0:T(8,128)S(1)}, u32[]{:S(2)}) copy-start(f32[1024,2304]{1,0:T(8,128)S(1)} %get-tuple-element.52) | copy-start | bytes 28311556
  146.8 0.9 copy-start.4
  178.3 60.8 %copy-start.1 = (bf16[3,2304,64]{1,2,0:T(8,128)(2,1)S(1)}, bf16[3,2304,64]{1,2,0:T(8,128)(2,1)}, u32[]{:S(2)}) copy-start(bf16[3,2304,64]{1,2,0:T(8,128)(2,1)} %param.13) | copy-start | bytes 2654212
Sparse Core Ops, SparseCore 0:
  9.7 54.3 all-gather.4
  78.6 35.4 all-gather.8
  116.1 20.9 all-gather.6
  182.1 54.5 reduce-scatter.1
